TPU v7x, 128 devices: a whole 4x4x4 slice. The times are simulated.
128 devices in a mesh: batch: 4 (over x), seq: 32 (over y, z, core).
Axes of the slice: x: 4, y: 4, z: 4, core: 2. Of those that a mesh axis runs over, the one named last changes fastest.
Arguments:
- tokens: bfloat16 [65536, 512], P(('batch', 'seq')), parts along dimension 0, may hold values from -50 to 50
- w_query: bfloat16 [512, 512], replicated, may hold values from -0.25 to 0.25
- w_key: bfloat16 [512, 512], replicated, may hold values from -0.25 to 0.25
- w_value: bfloat16 [512, 512], replicated, may hold values from -0.25 to 0.25
- w_output: bfloat16 [512, 512], replicated, may hold values from -0.25 to 0.25
Outputs:
- mixed: bfloat16 [65536, 512], P(('batch', 'seq')), parts along dimension 0
There are 4 independent parts, one for each index of `batch`. A program takes and returns all parts, laid end to end along the dimension named above; an argument that names none is the same for every part. Nothing has to cross between parts.
All inputs are finite; a program needn't handle non-finite values.
Results may differ from a plain program's by a relative error of at most 0.0059.
The roundings to bfloat16 on the way count: a program that leaves them out, or rounds other values in their place, can miss the bound.
Values sent between devices are 32-bit elements; how exact they have to be, the bound alone decides.
No kernel may reach another device: no remote copies, remote signals or barrier semaphores. Data moves between devices by JAX's collectives and lax.ppermute only.
A program may use at most 192 MiB of HBM per device.

v0:
```python
import functools
import math

import jax
import jax.numpy as jnp
from jax import lax
from jax.experimental import pallas as pl
from jax.experimental.pallas import tpu as pltpu
from jax.sharding import PartitionSpec as P

HEADS = 8
HEAD_DIM = 64
BLK = 128
D = HEADS * HEAD_DIM
LN2 = math.log(2.0)
F32 = jnp.float32
BF16 = jnp.bfloat16
VMEM = pl.BlockSpec(memory_space=pltpu.VMEM)
PARAMS = pltpu.CompilerParams(vmem_limit_bytes=48 * 1024 * 1024)


def call(body, outs, *args, scratch=()):
    return pl.pallas_call(
        body,
        out_shape=outs,
        in_specs=[VMEM] * len(args),
        out_specs=jax.tree.map(lambda _: VMEM, outs),
        scratch_shapes=list(scratch),
        compiler_params=PARAMS,
    )(*args)


def shape(*dims, dtype=F32):
    return jax.ShapeDtypeStruct(dims, dtype)


def pool_matrix(rows, cols, level):
    row = lax.broadcasted_iota(jnp.int32, (rows, cols), 0)
    col = lax.broadcasted_iota(jnp.int32, (rows, cols), 1)
    return jnp.where((col >> level) == row, 2.0**-level, 0.0).astype(BF16)


def project_kernel(x_ref, wk_ref, wv_ref, k_ref, v_ref, *coarse_refs):
    x = x_ref[...]
    for half, (w_ref, r_ref) in enumerate(((wk_ref, k_ref), (wv_ref, v_ref))):
        r_ref[...] = jnp.dot(x, w_ref[...], preferred_element_type=F32).astype(BF16)
    rows = x.shape[0]
    levels = [2, 3, 4, 5, 6]
    for level, ref in zip(levels, coarse_refs):
        pool = pool_matrix(rows >> level, rows, level)
        for half, r_ref in enumerate((k_ref, v_ref)):
            ref[:, half * D : (half + 1) * D] = jnp.dot(
                pool, r_ref[...], preferred_element_type=F32
            )


def term(keys, query, value_t):
    scores = jnp.dot(keys, query, preferred_element_type=F32)
    top = jnp.max(scores, axis=0, keepdims=True)
    weights = jnp.exp(scores - top)
    denom = jnp.sum(weights, axis=0, keepdims=True)
    numer = jnp.dot(value_t, weights.astype(BF16), preferred_element_type=F32)
    return top, denom, numer


def merge(parts):
    common = functools.reduce(jnp.maximum, [p[0] for p in parts])
    factors = [jnp.exp(p[0] - common) for p in parts]
    denom = sum(p[1] * f for p, f in zip(parts, factors))
    numer = sum(p[2] * f for p, f in zip(parts, factors))
    return common, denom, numer


def local_kernel(x_ref, wq_ref, k_ref, v_ref, q_ref, top_ref, den_ref, acc_ref, vt_ref, k1_ref, v1t_ref):
    rows = x_ref.shape[0]
    q = jnp.dot(x_ref[...], wq_ref[...], preferred_element_type=F32).astype(BF16)
    qt = (q.astype(F32) * 0.125).T
    row = lax.broadcasted_iota(jnp.int32, (D, rows), 0)
    even = (row & HEAD_DIM) == 0
    q_ref[0] = jnp.where(even, qt, 0.0).astype(BF16)
    q_ref[1] = jnp.where(even, 0.0, qt).astype(BF16)
    vt_ref[...] = v_ref[...].astype(F32).T.astype(BF16)
    pool = pool_matrix(rows // 2, rows, 1)
    k1_ref[...] = jnp.dot(pool, k_ref[...], preferred_element_type=F32).astype(BF16)
    v1 = jnp.dot(pool, v_ref[...], preferred_element_type=F32)
    v1t_ref[...] = v1.T.astype(BF16)
    for head in range(HEADS):
        pair = slice(head // 2 * 128, head // 2 * 128 + 128)
        own = slice(head * HEAD_DIM, (head + 1) * HEAD_DIM)
        for block in range(rows // BLK):
            cols = slice(block * BLK, (block + 1) * BLK)
            query = q_ref[head % 2, pair, cols]
            parts = []
            for other in (block, block ^ 1):
                span = slice(other * BLK, (other + 1) * BLK)
                parts.append(term(k_ref[span, pair], query, vt_ref[own, span]))
            far = 1 - block // 2
            span = slice(far * BLK, (far + 1) * BLK)
            top, denom, numer = term(k1_ref[span, pair], query, v1t_ref[own, span])
            parts.append((top + LN2, denom, numer))
            top, denom, numer = merge(parts)
            top_ref[head : head + 1, cols] = top
            den_ref[head : head + 1, cols] = denom
            acc_ref[own, cols] = numer


def gather_rows(refs, pieces):
    return [refs[i][lo : lo + n, :] for i, lo, n in pieces]


def stage(refs, plan, kc_ref, vct_ref):
    for slot, pieces in enumerate(plan):
        rows = jnp.concatenate(gather_rows(refs, pieces), axis=0)
        kc_ref[slot] = rows[:, :D].astype(BF16)
        vct_ref[slot] = rows[:, D:].T.astype(BF16)


def remote_terms(head, q_ref, kc_ref, vct_ref, levels):
    pair = slice(head // 2 * 128, head // 2 * 128 + 128)
    own = slice(head * HEAD_DIM, (head + 1) * HEAD_DIM)
    parts = []
    for slot, level in enumerate(levels):
        top, denom, numer = term(
            kc_ref[slot, :, pair], q_ref[head % 2, pair, :], vct_ref[slot, own, :]
        )
        parts.append((top + level * LN2, denom, numer))
    return parts


def middle_kernel(plan, levels, n, *refs):
    rows, (q_ref, top_in, den_in, acc_in) = refs[:n], refs[n : n + 4]
    top_ref, den_ref, acc_ref, kc_ref, vct_ref = refs[n + 4 :]
    stage(rows, plan, kc_ref, vct_ref)
    for head in range(HEADS):
        own = slice(head * HEAD_DIM, (head + 1) * HEAD_DIM)
        parts = remote_terms(head, q_ref, kc_ref, vct_ref, levels)
        parts.append((top_in[head : head + 1, :], den_in[head : head + 1, :], acc_in[own, :]))
        top, denom, numer = merge(parts)
        top_ref[head : head + 1, :] = top
        den_ref[head : head + 1, :] = denom
        acc_ref[own, :] = numer


def final_kernel(plan, levels, n, *refs):
    rows, (q_ref, top_in, den_in, acc_in, wo_ref) = refs[:n], refs[n : n + 5]
    out_ref, kc_ref, vct_ref, att_ref = refs[n + 5 :]
    stage(rows, plan, kc_ref, vct_ref)
    for head in range(HEADS):
        own = slice(head * HEAD_DIM, (head + 1) * HEAD_DIM)
        parts = remote_terms(head, q_ref, kc_ref, vct_ref, levels)
        parts.append((top_in[head : head + 1, :], den_in[head : head + 1, :], acc_in[own, :]))
        _, denom, numer = merge(parts)
        att_ref[own, :] = numer / denom
    att = att_ref[...].T.astype(BF16)
    out_ref[...] = jnp.dot(att, wo_ref[...], preferred_element_type=F32).astype(BF16)


def shards(tokens, w_query, w_key, w_value, w_output):
    rows = tokens.shape[0]
    count = lax.axis_size("seq")

    def swap(block, apart):
        return lax.ppermute(block, "seq", [(i, i ^ apart) for i in range(count)])

    k, v, c2, c3, c4, c5, c6 = call(
        project_kernel,
        [shape(rows, D, dtype=BF16)] * 2 + [shape(rows >> l, 2 * D) for l in range(2, 7)],
        tokens,
        w_key,
        w_value,
    )
    y1, y2, y3 = swap(c5, 8), swap(c6, 16), swap(c6, 24)
    s2 = swap(c2, 1)
    z1, z2, z3 = swap(c3, 2), swap(c4, 4), swap(c4, 6)
    g = jnp.concatenate([y1, y2, y3], axis=0)
    g1, g2, g3 = swap(g, 2), swap(g, 4), swap(g, 6)
    near = swap(jnp.concatenate([z1, z2, z3], axis=0), 1)
    far = swap(jnp.concatenate([g, g1, g2, g3], axis=0), 1)

    state = [shape(HEADS, rows), shape(HEADS, rows), shape(D, rows)]
    q, top, den, acc = call(
        local_kernel,
        [shape(2, D, rows, dtype=BF16)] + state,
        tokens,
        w_query,
        k,
        v,
        scratch=[
            pltpu.VMEM((D, rows), BF16),
            pltpu.VMEM((rows // 2, D), BF16),
            pltpu.VMEM((D, rows // 2), BF16),
        ],
    )

    def staged(slots):
        return [pltpu.VMEM((slots, BLK, D), BF16), pltpu.VMEM((slots, D, BLK), BF16)]

    arrays = [s2, z1, z2, z3, near]
    plan = [[(0, 0, 128)], [(1, 0, 64), (4, 0, 64)], [(2, 0, 32), (3, 0, 32), (4, 64, 64)]]
    top, den, acc = call(
        functools.partial(middle_kernel, plan, (2, 3, 4), len(arrays)),
        state,
        *arrays,
        q,
        top,
        den,
        acc,
        scratch=staged(3),
    )
    arrays = [g, g1, g2, g3, far]
    plan = [
        [(i, 0, 16) for i in range(4)] + [(4, 32 * i, 16) for i in range(4)],
        [(i, 16, 16) for i in range(4)] + [(4, 32 * i + 16, 16) for i in range(4)],
    ]
    return call(
        functools.partial(final_kernel, plan, (5, 6), len(arrays)),
        shape(rows, D, dtype=BF16),
        *arrays,
        q,
        top,
        den,
        acc,
        w_output,
        scratch=staged(2) + [pltpu.VMEM((D, rows), F32)],
    )


def solution(mesh):
    return jax.shard_map(
        shards,
        mesh=mesh,
        in_specs=(P(("batch", "seq"), None), P(), P(), P(), P()),
        out_specs=P(("batch", "seq"), None),
        check_vma=False,
    )
```

profile of v0, /device:TPU:1, one launch (start us, length us, event | category | flops | bytes accessed | tf_op | source)
XLA Modules:
  0.0 52.7 jit_solution(5918386941492849372)
XLA Ops:
  0.0 1.0 %copy-done = bf16[512,512]{1,0:T(8,128)(2,1)S(1)} copy-done((bf16[512,512]{1,0:T(8,128)(2,1)S(1)}, bf16[512,512]{1,0:T(8,128)(2,1)}, u32[]{:S(2)}) %copy-start) | copy-done | bytes 524312
  1.0 1.0 %copy-done.1 = bf16[512,512]{1,0:T(8,128)(2,1)S(1)} copy-done((bf16[512,512]{1,0:T(8,128)(2,1)S(1)}, bf16[512,512]{1,0:T(8,128)(2,1)}, u32[]{:S(2)}) %copy-start.1) | copy-done | bytes 524312
  2.1 1.0 %copy-done.2 = bf16[512,512]{1,0:T(8,128)(2,1)S(1)} copy-done((bf16[512,512]{1,0:T(8,128)(2,1)S(1)}, bf16[512,512]{1,0:T(8,128)(2,1)}, u32[]{:S(2)}) %copy-start.2) | copy-done | bytes 524312
  3.1 1.5 %shard_map.55 = (bf16[512,512]{1,0:T(8,128)(2,1)S(1)}, bf16[512,512]{1,0:T(8,128)(2,1)S(1)}, f32[128,1024]{1,0:T(8,128)S(1)}, f32[64,1024]{1,0:T(8,128)S(1)}, f3...) custom-call(bf16[512,512]{1,0:T(8,128)(2,1)S(1)} %copy-done, bf16[512,512]{1,0:T(8,128)(2,1)S(1)} %copy-done.1, ...), custom_call_target="tpu_custom_call" | custom-call | tf_op jit(solution)/shard_map/pallas_call | solution.py:23
  4.6 2.1 %collective-permute-start = (f32[16,1024]{1,0:T(8,128)S(1)}, f32[16,1024]{1,0:T(8,128)S(1)}, u32[]{:S(2)}, u32[]{:S(2)}) collective-permute-start(f32[16,1024]{1,0:T(8,128)S(1)} %get-tuple-element.19), channel_id=1, source_target_pairs={{0,8},{1,9},{2,10},{3,11},{4,12},{5,13},{6,14},{7,15},{8,0},{9,1},... | collective-permute-start | bytes 196616 | tf_op jit(solution)/shard_map/ppermute | solution.py:163
  6.7 2.6 %collective-permute-start.1 = (f32[8,1024]{1,0:T(8,128)S(1)}, f32[8,1024]{1,0:T(8,128)S(1)}, u32[]{:S(2)}, u32[]{:S(2)}) collective-permute-start(f32[8,1024]{1,0:T(8,128)S(1)} %get-tuple-element.20), channel_id=1, source_target_pairs={{0,16},{1,17},{2,18},{3,19},{4,20},{5,21},{6,22},{7,23},{8,24},{9,... | collective-permute-start | bytes 98312 | tf_op jit(solution)/shard_map/ppermute | solution.py:163
  9.3 0.0 collective-permute-start.2
  9.3 0.0 collective-permute-done
  9.4 2.0 %collective-permute-done.1 = f32[8,1024]{1,0:T(8,128)S(1)} collective-permute-done((f32[8,1024]{1,0:T(8,128)S(1)}, f32[8,1024]{1,0:T(8,128)S(1)}, u32[]{:S(2)}, u32[]{:S(2)}) %collective-permute-start.1) | collective-permute-done | bytes 32800 | tf_op jit(solution)/shard_map/ppermute | solution.py:163
  11.3 2.0 %collective-permute-done.2 = f32[8,1024]{1,0:T(8,128)S(1)} collective-permute-done((f32[8,1024]{1,0:T(8,128)S(1)}, f32[8,1024]{1,0:T(8,128)S(1)}, u32[]{:S(2)}, u32[]{:S(2)}) %collective-permute-start.2) | collective-permute-done | bytes 32800 | tf_op jit(solution)/shard_map/ppermute | solution.py:163
  13.3 1.6 %collective-permute-start.3 = (f32[32,1024]{1,0:T(8,128)S(1)}, f32[32,1024]{1,0:T(8,128)S(1)}, u32[]{:S(2)}, u32[]{:S(2)}) collective-permute-start(f32[32,1024]{1,0:T(8,128)S(1)} %get-tuple-element.36.refs_0_), channel_id=1, source_target_pairs={{0,2},{1,3},{2,0},{3,1},{4,6},{5,7},{6,4},{7,5},{8,10},{9,11},{10,... | collective-permute-start | bytes 393224 | tf_op jit(solution)/shard_map/ppermute | solution.py:163
  15.0 0.1 collective-permute-start.8
  15.0 3.3 %collective-permute-start.4 = (f32[32,1024]{1,0:T(8,128)S(1)}, f32[32,1024]{1,0:T(8,128)S(1)}, u32[]{:S(2)}, u32[]{:S(2)}) collective-permute-start(f32[32,1024]{1,0:T(8,128)S(1)} %get-tuple-element.36.refs_0_), channel_id=1, source_target_pairs={{0,4},{1,5},{2,6},{3,7},{4,0},{5,1},{6,2},{7,3},{8,12},{9,13},{10,... | collective-permute-start | bytes 393224 | tf_op jit(solution)/shard_map/ppermute | solution.py:163
  18.4 0.4 collective-permute-start.10
  18.8 2.1 %collective-permute-start.9 = (f32[32,1024]{1,0:T(8,128)S(1)}, f32[32,1024]{1,0:T(8,128)S(1)}, u32[]{:S(2)}, u32[]{:S(2)}) collective-permute-start(f32[32,1024]{1,0:T(8,128)S(1)} %get-tuple-element.26), channel_id=1, source_target_pairs={{0,4},{1,5},{2,6},{3,7},{4,0},{5,1},{6,2},{7,3},{8,12},{9,13},{10,... | collective-permute-start | bytes 393224 | tf_op jit(solution)/shard_map/ppermute | solution.py:163
  20.9 0.0 collective-permute-done.3.refs_1_
  20.9 3.8 %collective-permute-start.7 = (f32[128,1024]{1,0:T(8,128)S(1)}, f32[128,1024]{1,0:T(8,128)S(1)}, u32[]{:S(2)}, u32[]{:S(2)}) collective-permute-start(f32[128,1024]{1,0:T(8,128)S(1)} %get-tuple-element.24), channel_id=1, source_target_pairs={{0,1},{1,0},{2,3},{3,2},{4,5},{5,4},{6,7},{7,6},{8,9},{9,8},{10,11... | collective-permute-start | bytes 1572872 | tf_op jit(solution)/shard_map/ppermute | solution.py:163
  24.7 2.8 %collective-permute-done.4.refs_2_ = f32[32,1024]{1,0:T(8,128)S(1)} collective-permute-done((f32[32,1024]{1,0:T(8,128)S(1)}, f32[32,1024]{1,0:T(8,128)S(1)}, u32[]{:S(2)}, u32[]{:S(2)}) %collective-permute-start.4) | collective-permute-done | bytes 131104 | tf_op jit(solution)/shard_map/ppermute | solution.py:163
  27.5 0.0 collective-permute-start.5
  27.6 0.0 copy-start.3
  27.6 0.0 collective-permute-done.10.refs_3_
  27.6 2.8 %collective-permute-done.9.refs_2_ = f32[32,1024]{1,0:T(8,128)S(1)} collective-permute-done((f32[32,1024]{1,0:T(8,128)S(1)}, f32[32,1024]{1,0:T(8,128)S(1)}, u32[]{:S(2)}, u32[]{:S(2)}) %collective-permute-start.9) | collective-permute-done | bytes 131104 | tf_op jit(solution)/shard_map/ppermute | solution.py:163
  30.3 0.0 collective-permute-done.8.refs_1_
  30.4 3.8 %collective-permute-start.11 = (f32[128,1024]{1,0:T(8,128)S(1)}, f32[128,1024]{1,0:T(8,128)S(1)}, u32[]{:S(2)}, u32[]{:S(2)}) collective-permute-start(f32[128,1024]{1,0:T(8,128)S(1)} %pad_maximum_fusion), channel_id=1, source_target_pairs={{0,1},{1,0},{2,3},{3,2},{4,5},{5,4},{6,7},{7,6},{8,9},{9,8},{10,11... | collective-permute-start | bytes 1572872 | tf_op jit(solution)/shard_map/ppermute | solution.py:163
  34.2 0.5 collective-permute-done.5.refs_3_
  34.7 4.4 %collective-permute-start.6 = (f32[128,1024]{1,0:T(8,128)S(1)}, f32[128,1024]{1,0:T(8,128)S(1)}, u32[]{:S(2)}, u32[]{:S(2)}) collective-permute-start(f32[128,1024]{1,0:T(8,128)S(1)} %constant_dynamic-update-slice_fusion.3), channel_id=1, source_target_pairs={{0,1},{1,0},{2,3},{3,2},{4,5},{5,4},{6,7},{7,6},{8,9},{9,8},{10,11... | collective-permute-start | bytes 1572872 | tf_op jit(solution)/shard_map/ppermute | solution.py:163
  39.1 2.7 %shard_map.56 = (bf16[2,512,512]{2,1,0:T(8,128)(2,1)S(1)}, f32[8,512]{1,0:T(8,128)S(1)}, f32[8,512]{1,0:T(8,128)S(1)}, f32[512,512]{1,0:T(8,128)S(1)}) custom-call(bf16[512,512]{1,0:T(8,128)(2,1)S(1)} %copy-done, bf16[512,512]{1,0:T(8,128)(2,1)S(1)} %copy-done.3, bf16[512,512]{1,0:T(8,128)(2,1)S(1)} %get-tuple-element.21.k_ref, ...), custom_call_target="tpu_custom_call" | custom-call | tf_op jit(solution)/shard_map/pallas_call | solution.py:23
  41.7 0.0 collective-permute-done.7.refs_0_
  41.8 0.0 collective-permute-done.11.refs_4_
  41.8 0.0 copy-start.4
  41.8 5.9 %shard_map.57 = (f32[8,512]{1,0:T(8,128)S(1)}, f32[8,512]{1,0:T(8,128)S(1)}, f32[512,512]{1,0:T(8,128)S(1)}) custom-call(f32[128,1024]{1,0:T(8,128)S(1)} %collective-permute-done.7.refs_0_, f32[64,1024]{1,0:T(8,128)S(1)} %collective-permute-done.8.refs_1_, f32[32,1024]{1,0:T(8,128)S(1)} %collective-permute-done.9.refs_2_, ...), custom_call_target="tpu_custom_call" | custom-call | tf_op jit(solution)/shard_map/pallas_call | solution.py:23
  47.7 5.1 %shard_map.58 = bf16[512,512]{1,0:T(8,128)(2,1)} custom-call(f32[32,1024]{1,0:T(8,128)S(1)} %get-tuple-element.36.refs_0_, f32[32,1024]{1,0:T(8,128)S(1)} %collective-permute-done.3.refs_1_, f32[32,1024]{1,0:T(8,128)S(1)} %collective-permute-done.4.refs_2_, f32[32,1024]{1,0:T(8,128)S(1)} %collective-permute-done.5.refs_3_, ...), custom_call_target="tpu_custom_call" | custom-call | tf_op jit(solution)/shard_map/pallas_call | solution.py:23
  (13 shorter events, 0.1 us)
Async XLA Ops:
  0.0 1.0 %copy-start = (bf16[512,512]{1,0:T(8,128)(2,1)S(1)}, bf16[512,512]{1,0:T(8,128)(2,1)}, u32[]{:S(2)}) copy-start(bf16[512,512]{1,0:T(8,128)(2,1)} %x_ref.3) | copy-start | bytes 1572868
  1.0 1.0 %copy-start.1 = (bf16[512,512]{1,0:T(8,128)(2,1)S(1)}, bf16[512,512]{1,0:T(8,128)(2,1)}, u32[]{:S(2)}) copy-start(bf16[512,512]{1,0:T(8,128)(2,1)} %wk_ref.1) | copy-start | bytes 1572868
  2.1 1.0 %copy-start.2 = (bf16[512,512]{1,0:T(8,128)(2,1)S(1)}, bf16[512,512]{1,0:T(8,128)(2,1)}, u32[]{:S(2)}) copy-start(bf16[512,512]{1,0:T(8,128)(2,1)} %wv_ref.1) | copy-start | bytes 1572868
  4.6 4.8 %collective-permute-start = (f32[16,1024]{1,0:T(8,128)S(1)}, f32[16,1024]{1,0:T(8,128)S(1)}, u32[]{:S(2)}, u32[]{:S(2)}) collective-permute-start(f32[16,1024]{1,0:T(8,128)S(1)} %get-tuple-element.19), channel_id=1, source_target_pairs={{0,8},{1,9},{2,10},{3,11},{4,12},{5,13},{6,14},{7,15},{8,0},{9,1},... | collective-permute-start | bytes 196616 | tf_op jit(solution)/shard_map/ppermute | solution.py:163
  6.7 4.6 %collective-permute-start.1 = (f32[8,1024]{1,0:T(8,128)S(1)}, f32[8,1024]{1,0:T(8,128)S(1)}, u32[]{:S(2)}, u32[]{:S(2)}) collective-permute-start(f32[8,1024]{1,0:T(8,128)S(1)} %get-tuple-element.20), channel_id=1, source_target_pairs={{0,16},{1,17},{2,18},{3,19},{4,20},{5,21},{6,22},{7,23},{8,24},{9,... | collective-permute-start | bytes 98312 | tf_op jit(solution)/shard_map/ppermute | solution.py:163
  9.3 4.0 %collective-permute-start.2 = (f32[8,1024]{1,0:T(8,128)S(1)}, f32[8,1024]{1,0:T(8,128)S(1)}, u32[]{:S(2)}, u32[]{:S(2)}) collective-permute-start(f32[8,1024]{1,0:T(8,128)S(1)} %get-tuple-element.20), channel_id=1, source_target_pairs={{0,24},{1,25},{2,26},{3,27},{4,28},{5,29},{6,30},{7,31},{8,16},{9,... | collective-permute-start | bytes 98312 | tf_op jit(solution)/shard_map/ppermute | solution.py:163
  13.3 7.6 %collective-permute-start.3 = (f32[32,1024]{1,0:T(8,128)S(1)}, f32[32,1024]{1,0:T(8,128)S(1)}, u32[]{:S(2)}, u32[]{:S(2)}) collective-permute-start(f32[32,1024]{1,0:T(8,128)S(1)} %get-tuple-element.36.refs_0_), channel_id=1, source_target_pairs={{0,2},{1,3},{2,0},{3,1},{4,6},{5,7},{6,4},{7,5},{8,10},{9,11},{10,... | collective-permute-start | bytes 393224 | tf_op jit(solution)/shard_map/ppermute | solution.py:163
  15.0 15.4 %collective-permute-start.8 = (f32[64,1024]{1,0:T(8,128)S(1)}, f32[64,1024]{1,0:T(8,128)S(1)}, u32[]{:S(2)}, u32[]{:S(2)}) collective-permute-start(f32[64,1024]{1,0:T(8,128)S(1)} %get-tuple-element.25), channel_id=1, source_target_pairs={{0,2},{1,3},{2,0},{3,1},{4,6},{5,7},{6,4},{7,5},{8,10},{9,11},{10,... | collective-permute-start | bytes 786440 | tf_op jit(solution)/shard_map/ppermute | solution.py:163
  15.0 12.5 %collective-permute-start.4 = (f32[32,1024]{1,0:T(8,128)S(1)}, f32[32,1024]{1,0:T(8,128)S(1)}, u32[]{:S(2)}, u32[]{:S(2)}) collective-permute-start(f32[32,1024]{1,0:T(8,128)S(1)} %get-tuple-element.36.refs_0_), channel_id=1, source_target_pairs={{0,4},{1,5},{2,6},{3,7},{4,0},{5,1},{6,2},{7,3},{8,12},{9,13},{10,... | collective-permute-start | bytes 393224 | tf_op jit(solution)/shard_map/ppermute | solution.py:163
  18.4 9.2 %collective-permute-start.10 = (f32[32,1024]{1,0:T(8,128)S(1)}, f32[32,1024]{1,0:T(8,128)S(1)}, u32[]{:S(2)}, u32[]{:S(2)}) collective-permute-start(f32[32,1024]{1,0:T(8,128)S(1)} %get-tuple-element.26), channel_id=1, source_target_pairs={{0,6},{1,7},{2,4},{3,5},{4,2},{5,3},{6,0},{7,1},{8,14},{9,15},{10,... | collective-permute-start | bytes 393224 | tf_op jit(solution)/shard_map/ppermute | solution.py:163
  18.8 11.5 %collective-permute-start.9 = (f32[32,1024]{1,0:T(8,128)S(1)}, f32[32,1024]{1,0:T(8,128)S(1)}, u32[]{:S(2)}, u32[]{:S(2)}) collective-permute-start(f32[32,1024]{1,0:T(8,128)S(1)} %get-tuple-element.26), channel_id=1, source_target_pairs={{0,4},{1,5},{2,6},{3,7},{4,0},{5,1},{6,2},{7,3},{8,12},{9,13},{10,... | collective-permute-start | bytes 393224 | tf_op jit(solution)/shard_map/ppermute | solution.py:163
  20.9 20.8 %collective-permute-start.7 = (f32[128,1024]{1,0:T(8,128)S(1)}, f32[128,1024]{1,0:T(8,128)S(1)}, u32[]{:S(2)}, u32[]{:S(2)}) collective-permute-start(f32[128,1024]{1,0:T(8,128)S(1)} %get-tuple-element.24), channel_id=1, source_target_pairs={{0,1},{1,0},{2,3},{3,2},{4,5},{5,4},{6,7},{7,6},{8,9},{9,8},{10,11... | collective-permute-start | bytes 1572872 | tf_op jit(solution)/shard_map/ppermute | solution.py:163
  27.5 7.1 %collective-permute-start.5 = (f32[32,1024]{1,0:T(8,128)S(1)}, f32[32,1024]{1,0:T(8,128)S(1)}, u32[]{:S(2)}, u32[]{:S(2)}) collective-permute-start(f32[32,1024]{1,0:T(8,128)S(1)} %get-tuple-element.36.refs_0_), channel_id=1, source_target_pairs={{0,6},{1,7},{2,4},{3,5},{4,2},{5,3},{6,0},{7,1},{8,14},{9,15},{10,... | collective-permute-start | bytes 393224 | tf_op jit(solution)/shard_map/ppermute | solution.py:163
  27.6 11.5 %copy-start.3 = (bf16[512,512]{1,0:T(8,128)(2,1)S(1)}, bf16[512,512]{1,0:T(8,128)(2,1)}, u32[]{:S(2)}) copy-start(bf16[512,512]{1,0:T(8,128)(2,1)} %wq_ref.1) | copy-start | bytes 1572868
  30.4 11.4 %collective-permute-start.11 = (f32[128,1024]{1,0:T(8,128)S(1)}, f32[128,1024]{1,0:T(8,128)S(1)}, u32[]{:S(2)}, u32[]{:S(2)}) collective-permute-start(f32[128,1024]{1,0:T(8,128)S(1)} %pad_maximum_fusion), channel_id=1, source_target_pairs={{0,1},{1,0},{2,3},{3,2},{4,5},{5,4},{6,7},{7,6},{8,9},{9,8},{10,11... | collective-permute-start | bytes 1572872 | tf_op jit(solution)/shard_map/ppermute | solution.py:163
  34.7 13.0 %collective-permute-start.6 = (f32[128,1024]{1,0:T(8,128)S(1)}, f32[128,1024]{1,0:T(8,128)S(1)}, u32[]{:S(2)}, u32[]{:S(2)}) collective-permute-start(f32[128,1024]{1,0:T(8,128)S(1)} %constant_dynamic-update-slice_fusion.3), channel_id=1, source_target_pairs={{0,1},{1,0},{2,3},{3,2},{4,5},{5,4},{6,7},{7,6},{8,9},{9,8},{10,11... | collective-permute-start | bytes 1572872 | tf_op jit(solution)/shard_map/ppermute | solution.py:163
  41.8 5.9 %copy-start.4 = (bf16[512,512]{1,0:T(8,128)(2,1)S(1)}, bf16[512,512]{1,0:T(8,128)(2,1)}, u32[]{:S(2)}) copy-start(bf16[512,512]{1,0:T(8,128)(2,1)} %refs_9_.1) | copy-start | bytes 1572868
where the time goes:
time: 53 us; the launch traced here: 52.7 us
  starting transfers between devices  24.3 us (46%)
  Pallas kernels  15.1 us (28%)
  waiting for transfers between devices  10 us (19%)
  local copies, waits for them, and re-layouts  3.19 us (6%)
    ppermute x12, starting transfers between devices, swap(): return lax.ppermute(block, 'seq', [(i, i ^ apart) for i in range(count)])  24.3 us
    pallas_call x4, Pallas kernels, call(): pl.pallas_call(body, out_shape=outs, in_specs=[VMEM] * len(args), out_spe...  15.1 us
    ppermute x12, waiting for transfers between devices, swap(): return lax.ppermute(block, 'seq', [(i, i ^ apart) for i in range(count)])  10 us
    unnamed x15, local copies, waits for them, and re-layouts  3.18 us
  transfers between devices with their start and end apart: 12, of which 5 were waited for; matrix products, arithmetic and copies ran while one was open for 0% of the time, Pallas kernels for 16%

commit v1 on v0

--- a/solution.py
+++ b/solution.py
@@ -19,11 +19,11 @@
 PARAMS = pltpu.CompilerParams(vmem_limit_bytes=48 * 1024 * 1024)
 
 
-def call(body, outs, *args, scratch=()):
+def call(body, outs, *args, scratch=(), place=VMEM):
     return pl.pallas_call(
         body,
         out_shape=outs,
-        in_specs=[VMEM] * len(args),
+        in_specs=[place] * len(args),
         out_specs=jax.tree.map(lambda _: VMEM, outs),
         scratch_shapes=list(scratch),
         compiler_params=PARAMS,
@@ -40,11 +40,19 @@
     return jnp.where((col >> level) == row, 2.0**-level, 0.0).astype(BF16)
 
 
-def project_kernel(x_ref, wk_ref, wv_ref, k_ref, v_ref, *coarse_refs):
-    x = x_ref[...]
-    for half, (w_ref, r_ref) in enumerate(((wk_ref, k_ref), (wv_ref, v_ref))):
-        r_ref[...] = jnp.dot(x, w_ref[...], preferred_element_type=F32).astype(BF16)
-    rows = x.shape[0]
+def project_kernel(x_hbm, wk_hbm, wv_hbm, k_ref, v_ref, *refs):
+    coarse_refs, (x_ref, wk_ref, wv_ref, sems) = refs[:5], refs[5:]
+    copies = [
+        pltpu.make_async_copy(src, dst, sems.at[i])
+        for i, (src, dst) in enumerate(((x_hbm, x_ref), (wk_hbm, wk_ref), (wv_hbm, wv_ref)))
+    ]
+    for copy in copies:
+        copy.start()
+    copies[0].wait()
+    for copy, w_ref, r_ref in ((copies[1], wk_ref, k_ref), (copies[2], wv_ref, v_ref)):
+        copy.wait()
+        r_ref[...] = jnp.dot(x_ref[...], w_ref[...], preferred_element_type=F32).astype(BF16)
+    rows = x_ref.shape[0]
     levels = [2, 3, 4, 5, 6]
     for level, ref in zip(levels, coarse_refs):
         pool = pool_matrix(rows >> level, rows, level)
@@ -115,42 +123,45 @@
         vct_ref[slot] = rows[:, D:].T.astype(BF16)
 
 
-def remote_terms(head, q_ref, kc_ref, vct_ref, levels):
+def remote_terms(head, cols, q_ref, kc_ref, vct_ref, levels):
     pair = slice(head // 2 * 128, head // 2 * 128 + 128)
     own = slice(head * HEAD_DIM, (head + 1) * HEAD_DIM)
     parts = []
     for slot, level in enumerate(levels):
         top, denom, numer = term(
-            kc_ref[slot, :, pair], q_ref[head % 2, pair, :], vct_ref[slot, own, :]
+            kc_ref[slot, :, pair], q_ref[head % 2, pair, cols], vct_ref[slot, own, :]
         )
         parts.append((top + level * LN2, denom, numer))
     return parts
+
+
+def chunks(rows):
+    for head in range(HEADS):
+        for lo in range(0, rows, BLK):
+            yield head, slice(head * HEAD_DIM, (head + 1) * HEAD_DIM), slice(lo, lo + BLK)
 
 
 def middle_kernel(plan, levels, n, *refs):
     rows, (q_ref, top_in, den_in, acc_in) = refs[:n], refs[n : n + 4]
     top_ref, den_ref, acc_ref, kc_ref, vct_ref = refs[n + 4 :]
     stage(rows, plan, kc_ref, vct_ref)
-    for head in range(HEADS):
-        own = slice(head * HEAD_DIM, (head + 1) * HEAD_DIM)
-        parts = remote_terms(head, q_ref, kc_ref, vct_ref, levels)
-        parts.append((top_in[head : head + 1, :], den_in[head : head + 1, :], acc_in[own, :]))
-        top, denom, numer = merge(parts)
-        top_ref[head : head + 1, :] = top
-        den_ref[head : head + 1, :] = denom
-        acc_ref[own, :] = numer
+    for head, own, cols in chunks(acc_ref.shape[1]):
+        parts = remote_terms(head, cols, q_ref, kc_ref, vct_ref, levels)
+        one = slice(head, head + 1)
+        parts.append((top_in[one, cols], den_in[one, cols], acc_in[own, cols]))
+        top_ref[one, cols], den_ref[one, cols], acc_ref[own, cols] = merge(parts)
 
 
 def final_kernel(plan, levels, n, *refs):
     rows, (q_ref, top_in, den_in, acc_in, wo_ref) = refs[:n], refs[n : n + 5]
     out_ref, kc_ref, vct_ref, att_ref = refs[n + 5 :]
     stage(rows, plan, kc_ref, vct_ref)
-    for head in range(HEADS):
-        own = slice(head * HEAD_DIM, (head + 1) * HEAD_DIM)
-        parts = remote_terms(head, q_ref, kc_ref, vct_ref, levels)
-        parts.append((top_in[head : head + 1, :], den_in[head : head + 1, :], acc_in[own, :]))
+    for head, own, cols in chunks(acc_in.shape[1]):
+        parts = remote_terms(head, cols, q_ref, kc_ref, vct_ref, levels)
+        one = slice(head, head + 1)
+        parts.append((top_in[one, cols], den_in[one, cols], acc_in[own, cols]))
         _, denom, numer = merge(parts)
-        att_ref[own, :] = numer / denom
+        att_ref[own, cols] = numer / denom
     att = att_ref[...].T.astype(BF16)
     out_ref[...] = jnp.dot(att, wo_ref[...], preferred_element_type=F32).astype(BF16)
 
@@ -165,18 +176,15 @@
     k, v, c2, c3, c4, c5, c6 = call(
         project_kernel,
         [shape(rows, D, dtype=BF16)] * 2 + [shape(rows >> l, 2 * D) for l in range(2, 7)],
-        tokens,
-        w_key,
-        w_value,
+        *(pltpu.with_memory_space_constraint(a, pltpu.HBM) for a in (tokens, w_key, w_value)),
+        scratch=[pltpu.VMEM((rows, D), BF16)]
+        + [pltpu.VMEM((D, D), BF16)] * 2
+        + [pltpu.SemaphoreType.DMA((3,))],
+        place=pl.BlockSpec(memory_space=pltpu.HBM),
     )
     y1, y2, y3 = swap(c5, 8), swap(c6, 16), swap(c6, 24)
     s2 = swap(c2, 1)
     z1, z2, z3 = swap(c3, 2), swap(c4, 4), swap(c4, 6)
-    g = jnp.concatenate([y1, y2, y3], axis=0)
-    g1, g2, g3 = swap(g, 2), swap(g, 4), swap(g, 6)
-    near = swap(jnp.concatenate([z1, z2, z3], axis=0), 1)
-    far = swap(jnp.concatenate([g, g1, g2, g3], axis=0), 1)
-
     state = [shape(HEADS, rows), shape(HEADS, rows), shape(D, rows)]
     q, top, den, acc = call(
         local_kernel,
@@ -191,7 +199,10 @@
             pltpu.VMEM((D, rows // 2), BF16),
         ],
     )
-
+    y1, y2, y3, z1, z2, z3, top = lax.optimization_barrier((y1, y2, y3, z1, z2, z3, top))
+    g = jnp.concatenate([y1, y2, y3], axis=0)
+    g1, g2, g3 = swap(g, 2), swap(g, 4), swap(g, 6)
+    near = swap(jnp.concatenate([z1, z2, z3], axis=0), 1)
     def staged(slots):
         return [pltpu.VMEM((slots, BLK, D), BF16), pltpu.VMEM((slots, D, BLK), BF16)]
 
@@ -207,11 +218,11 @@
         acc,
         scratch=staged(3),
     )
-    arrays = [g, g1, g2, g3, far]
-    plan = [
-        [(i, 0, 16) for i in range(4)] + [(4, 32 * i, 16) for i in range(4)],
-        [(i, 16, 16) for i in range(4)] + [(4, 32 * i + 16, 16) for i in range(4)],
-    ]
+    f0 = swap(g, 1)
+    g1, g2, g3, top = lax.optimization_barrier((g1, g2, g3, top))
+    f1, f2, f3 = [swap(part, 1) for part in (g1, g2, g3)]
+    arrays = [g, g1, g2, g3, f0, f1, f2, f3]
+    plan = [[(i, lo, 16) for i in range(8)] for lo in (0, 16)]
     return call(
         functools.partial(final_kernel, plan, (5, 6), len(arrays)),
         shape(rows, D, dtype=BF16),

time: 53 us -> 39.5 us (0.75)
  Pallas kernels: 15.1 us -> 10.2 us
  local copies, waits for them, and re-layouts: 3.19 us -> 0.03 us
  waiting for transfers between devices: 10 us -> 7.32 us
  starting transfers between devices: 24.3 us -> 21.7 us
    pallas_call x4, Pallas kernels: 15.1 us -> 10.2 us  [call(): pl.pallas_call(body, out_shape=outs, in_specs=[place] * len(args), out_sp...]
    unnamed x15 -> x8, local copies, waits for them, and re-layouts: 3.18 us -> 0.02 us
    ppermute x12 -> x15, waiting for transfers between devices: 10 us -> 7.32 us  [swap(): return lax.ppermute(block, 'seq', [(i, i ^ apart) for i in range(count)])]
    ppermute x12 -> x15, starting transfers between devices: 24.3 us -> 21.7 us  [swap(): return lax.ppermute(block, 'seq', [(i, i ^ apart) for i in range(count)])]
  transfers between devices with their start and end apart: 12 -> 15, of which waited for: 5 -> 6; matrix products, arithmetic and copies ran while one was open for 0% -> 0% of each run, Pallas kernels for 16% -> 12%
where the time goes in v1:
time: 39.5 us; the launch traced here: 39.3 us
  starting transfers between devices  21.7 us (55%)
  Pallas kernels  10.2 us (26%)
  waiting for transfers between devices  7.32 us (19%)
    ppermute x15, starting transfers between devices, swap(): return lax.ppermute(block, 'seq', [(i, i ^ apart) for i in range(count)])  21.7 us
    pallas_call x4, Pallas kernels, call(): pl.pallas_call(body, out_shape=outs, in_specs=[place] * len(args), out_sp...  10.2 us
    ppermute x15, waiting for transfers between devices, swap(): return lax.ppermute(block, 'seq', [(i, i ^ apart) for i in range(count)])  7.32 us
  transfers between devices with their start and end apart: 15, of which 6 were waited for; matrix products, arithmetic and copies ran while one was open for 0% of the time, Pallas kernels for 12%

profile of v1, /device:TPU:1, one launch (start us, length us, event | category | flops | bytes accessed | tf_op | source)
XLA Modules:
  0.0 39.3 jit_solution(3507939618339680813)
XLA Ops:
  0.0 2.9 %shard_map.55 = (bf16[512,512]{1,0:T(8,128)(2,1)S(1)}, bf16[512,512]{1,0:T(8,128)(2,1)S(1)}, f32[128,1024]{1,0:T(8,128)S(1)}, f32[64,1024]{1,0:T(8,128)S(1)}, f3...) custom-call(bf16[512,512]{1,0:T(8,128)(2,1)} %x_ref.1, bf16[512,512]{1,0:T(8,128)(2,1)} %wk_hbm.1, ...), custom_call_target="tpu_custom_call" | custom-call | tf_op jit(solution)/shard_map/pallas_call | solution.py:23
  3.0 2.5 %collective-permute-start.3 = (f32[64,1024]{1,0:T(8,128)S(1)}, f32[64,1024]{1,0:T(8,128)S(1)}, u32[]{:S(2)}, u32[]{:S(2)}) collective-permute-start(f32[64,1024]{1,0:T(8,128)S(1)} %get-tuple-element.32), channel_id=1, source_target_pairs={{0,2},{1,3},{2,0},{3,1},{4,6},{5,7},{6,4},{7,5},{8,10},{9,11},{10,... | collective-permute-start | bytes 786440 | tf_op jit(solution)/shard_map/ppermute | solution.py:174
  5.5 3.3 %collective-permute-start.4 = (f32[32,1024]{1,0:T(8,128)S(1)}, f32[32,1024]{1,0:T(8,128)S(1)}, u32[]{:S(2)}, u32[]{:S(2)}) collective-permute-start(f32[32,1024]{1,0:T(8,128)S(1)} %get-tuple-element.33), channel_id=1, source_target_pairs={{0,4},{1,5},{2,6},{3,7},{4,0},{5,1},{6,2},{7,3},{8,12},{9,13},{10,... | collective-permute-start | bytes 393224 | tf_op jit(solution)/shard_map/ppermute | solution.py:174
  8.8 0.0 collective-permute-start.5
  8.8 2.9 %collective-permute-start.1 = (f32[8,1024]{1,0:T(8,128)S(1)}, f32[8,1024]{1,0:T(8,128)S(1)}, u32[]{:S(2)}, u32[]{:S(2)}) collective-permute-start(f32[8,1024]{1,0:T(8,128)S(1)} %get-tuple-element.31), channel_id=1, source_target_pairs={{0,16},{1,17},{2,18},{3,19},{4,20},{5,21},{6,22},{7,23},{8,24},{9,... | collective-permute-start | bytes 98312 | tf_op jit(solution)/shard_map/ppermute | solution.py:174
  11.7 0.4 %collective-permute-start = (f32[16,1024]{1,0:T(8,128)S(1)}, f32[16,1024]{1,0:T(8,128)S(1)}, u32[]{:S(2)}, u32[]{:S(2)}) collective-permute-start(f32[16,1024]{1,0:T(8,128)S(1)} %get-tuple-element.30), channel_id=1, source_target_pairs={{0,8},{1,9},{2,10},{3,11},{4,12},{5,13},{6,14},{7,15},{8,0},{9,1},... | collective-permute-start | bytes 196616 | tf_op jit(solution)/shard_map/ppermute | solution.py:174
  12.1 1.0 %collective-permute-done.1 = f32[8,1024]{1,0:T(8,128)S(1)} collective-permute-done((f32[8,1024]{1,0:T(8,128)S(1)}, f32[8,1024]{1,0:T(8,128)S(1)}, u32[]{:S(2)}, u32[]{:S(2)}) %collective-permute-start.1) | collective-permute-done | bytes 32800 | tf_op jit(solution)/shard_map/ppermute | solution.py:174
  13.1 2.7 %collective-permute-start.2 = (f32[8,1024]{1,0:T(8,128)S(1)}, f32[8,1024]{1,0:T(8,128)S(1)}, u32[]{:S(2)}, u32[]{:S(2)}) collective-permute-start(f32[8,1024]{1,0:T(8,128)S(1)} %get-tuple-element.31), channel_id=1, source_target_pairs={{0,24},{1,25},{2,26},{3,27},{4,28},{5,29},{6,30},{7,31},{8,16},{9,... | collective-permute-start | bytes 98312 | tf_op jit(solution)/shard_map/ppermute | solution.py:174
  15.8 2.7 %shard_map.56 = (bf16[2,512,512]{2,1,0:T(8,128)(2,1)S(1)}, f32[8,512]{1,0:T(8,128)S(1)}, f32[8,512]{1,0:T(8,128)S(1)}, f32[512,512]{1,0:T(8,128)S(1)}) custom-call(bf16[512,512]{1,0:T(8,128)(2,1)S(1)} %copy-done, bf16[512,512]{1,0:T(8,128)(2,1)S(1)} %copy-done.1, bf16[512,512]{1,0:T(8,128)(2,1)S(1)} %get-tuple-element.34.k_ref, ...), custom_call_target="tpu_custom_call" | custom-call | tf_op jit(solution)/shard_map/pallas_call | solution.py:23
  18.5 0.0 collective-permute-done.2
  18.5 2.8 %collective-permute-start.9 = (f32[128,1024]{1,0:T(8,128)S(1)}, f32[128,1024]{1,0:T(8,128)S(1)}, u32[]{:S(2)}, u32[]{:S(2)}) collective-permute-start(f32[128,1024]{1,0:T(8,128)S(1)} %get-tuple-element.40), channel_id=1, source_target_pairs={{0,1},{1,0},{2,3},{3,2},{4,5},{5,4},{6,7},{7,6},{8,9},{9,8},{10,11... | collective-permute-start | bytes 1572872 | tf_op jit(solution)/shard_map/ppermute | solution.py:174
  21.3 0.0 collective-permute-done
  21.3 0.0 collective-permute-done.4.refs_2_
  21.3 0.0 collective-permute-done.5.refs_3_
  21.3 0.0 collective-permute-done.3.refs_1_
  21.4 0.1 collective-permute-start.10
  21.5 0.1 collective-permute-start.6
  21.6 4.0 %collective-permute-start.7 = (f32[32,1024]{1,0:T(8,128)S(1)}, f32[32,1024]{1,0:T(8,128)S(1)}, u32[]{:S(2)}, u32[]{:S(2)}) collective-permute-start(f32[32,1024]{1,0:T(8,128)S(1)} %constant_dynamic-update-slice_fusion.refs_0_), channel_id=1, source_target_pairs={{0,4},{1,5},{2,6},{3,7},{4,0},{5,1},{6,2},{7,3},{8,12},{9,13},{10,... | collective-permute-start | bytes 393224 | tf_op jit(solution)/shard_map/ppermute | solution.py:174
  25.7 0.0 collective-permute-start.8
  25.7 0.0 collective-permute-done.9.refs_0_
  25.7 1.1 %collective-permute-start.11 = (f32[32,1024]{1,0:T(8,128)S(1)}, f32[32,1024]{1,0:T(8,128)S(1)}, u32[]{:S(2)}, u32[]{:S(2)}) collective-permute-start(f32[32,1024]{1,0:T(8,128)S(1)} %constant_dynamic-update-slice_fusion.refs_0_), channel_id=1, source_target_pairs={{0,1},{1,0},{2,3},{3,2},{4,5},{5,4},{6,7},{7,6},{8,9},{9,8},{10,11... | collective-permute-start | bytes 393224 | tf_op jit(solution)/shard_map/ppermute | solution.py:174
  26.8 2.0 %shard_map.57 = (f32[8,512]{1,0:T(8,128)S(1)}, f32[8,512]{1,0:T(8,128)S(1)}, f32[512,512]{1,0:T(8,128)S(1)}) custom-call(f32[128,1024]{1,0:T(8,128)S(1)} %collective-permute-done.9.refs_0_, f32[64,1024]{1,0:T(8,128)S(1)} %collective-permute-done.3.refs_1_, f32[32,1024]{1,0:T(8,128)S(1)} %collective-permute-done.4.refs_2_, ...), custom_call_target="tpu_custom_call" | custom-call | tf_op jit(solution)/shard_map/pallas_call | solution.py:23
  28.8 2.8 %collective-permute-done.7.refs_2_ = f32[32,1024]{1,0:T(8,128)S(1)} collective-permute-done((f32[32,1024]{1,0:T(8,128)S(1)}, f32[32,1024]{1,0:T(8,128)S(1)}, u32[]{:S(2)}, u32[]{:S(2)}) %collective-permute-start.7) | collective-permute-done | bytes 131104 | tf_op jit(solution)/shard_map/ppermute | solution.py:174
  31.6 2.5 %collective-permute-done.8.refs_3_ = f32[32,1024]{1,0:T(8,128)S(1)} collective-permute-done((f32[32,1024]{1,0:T(8,128)S(1)}, f32[32,1024]{1,0:T(8,128)S(1)}, u32[]{:S(2)}, u32[]{:S(2)}) %collective-permute-start.8) | collective-permute-done | bytes 131104 | tf_op jit(solution)/shard_map/ppermute | solution.py:174
  34.1 1.1 %collective-permute-start.12 = (f32[32,1024]{1,0:T(8,128)S(1)}, f32[32,1024]{1,0:T(8,128)S(1)}, u32[]{:S(2)}, u32[]{:S(2)}) collective-permute-start(f32[32,1024]{1,0:T(8,128)S(1)} %collective-permute-done.6.refs_1_), channel_id=1, source_target_pairs={{0,1},{1,0},{2,3},{3,2},{4,5},{5,4},{6,7},{7,6},{8,9},{9,8},{10,11... | collective-permute-start | bytes 393224 | tf_op jit(solution)/shard_map/ppermute | solution.py:174
  35.2 0.0 collective-permute-start.13
  35.2 0.5 %collective-permute-start.14 = (f32[32,1024]{1,0:T(8,128)S(1)}, f32[32,1024]{1,0:T(8,128)S(1)}, u32[]{:S(2)}, u32[]{:S(2)}) collective-permute-start(f32[32,1024]{1,0:T(8,128)S(1)} %collective-permute-done.8.refs_3_), channel_id=1, source_target_pairs={{0,1},{1,0},{2,3},{3,2},{4,5},{5,4},{6,7},{7,6},{8,9},{9,8},{10,11... | collective-permute-start | bytes 393224 | tf_op jit(solution)/shard_map/ppermute | solution.py:174
  35.7 0.0 collective-permute-done.11.refs_4_
  35.7 0.5 %collective-permute-done.12.refs_5_ = f32[32,1024]{1,0:T(8,128)S(1)} collective-permute-done((f32[32,1024]{1,0:T(8,128)S(1)}, f32[32,1024]{1,0:T(8,128)S(1)}, u32[]{:S(2)}, u32[]{:S(2)}) %collective-permute-start.12) | collective-permute-done | bytes 131104 | tf_op jit(solution)/shard_map/ppermute | solution.py:174
  36.2 0.4 collective-permute-done.13.refs_6_
  36.6 0.2 collective-permute-done.14.refs_7_
  36.8 2.6 %shard_map.58 = bf16[512,512]{1,0:T(8,128)(2,1)} custom-call(f32[32,1024]{1,0:T(8,128)S(1)} %constant_dynamic-update-slice_fusion.refs_0_, f32[32,1024]{1,0:T(8,128)S(1)} %collective-permute-done.6.refs_1_, f32[32,1024]{1,0:T(8,128)S(1)} %collective-permute-done.7.refs_2_, f32[32,1024]{1,0:T(8,128)S(1)} %collective-permute-done.8.refs_3_, ...), custom_call_target="tpu_custom_call" | custom-call | tf_op jit(solution)/shard_map/pallas_call | solution.py:23
  (12 shorter events, 0.1 us)
Async XLA Ops:
  0.0 15.8 %copy-start = (bf16[512,512]{1,0:T(8,128)(2,1)S(1)}, bf16[512,512]{1,0:T(8,128)(2,1)}, u32[]{:S(2)}) copy-start(bf16[512,512]{1,0:T(8,128)(2,1)} %x_ref.1) | copy-start | bytes 1572868
  0.0 15.8 %copy-start.1 = (bf16[512,512]{1,0:T(8,128)(2,1)S(1)}, bf16[512,512]{1,0:T(8,128)(2,1)}, u32[]{:S(2)}) copy-start(bf16[512,512]{1,0:T(8,128)(2,1)} %wq_ref.1) | copy-start | bytes 1572868
  3.0 18.4 %collective-permute-start.3 = (f32[64,1024]{1,0:T(8,128)S(1)}, f32[64,1024]{1,0:T(8,128)S(1)}, u32[]{:S(2)}, u32[]{:S(2)}) collective-permute-start(f32[64,1024]{1,0:T(8,128)S(1)} %get-tuple-element.32), channel_id=1, source_target_pairs={{0,2},{1,3},{2,0},{3,1},{4,6},{5,7},{6,4},{7,5},{8,10},{9,11},{10,... | collective-permute-start | bytes 786440 | tf_op jit(solution)/shard_map/ppermute | solution.py:174
  5.5 15.8 %collective-permute-start.4 = (f32[32,1024]{1,0:T(8,128)S(1)}, f32[32,1024]{1,0:T(8,128)S(1)}, u32[]{:S(2)}, u32[]{:S(2)}) collective-permute-start(f32[32,1024]{1,0:T(8,128)S(1)} %get-tuple-element.33), channel_id=1, source_target_pairs={{0,4},{1,5},{2,6},{3,7},{4,0},{5,1},{6,2},{7,3},{8,12},{9,13},{10,... | collective-permute-start | bytes 393224 | tf_op jit(solution)/shard_map/ppermute | solution.py:174
  8.8 12.5 %collective-permute-start.5 = (f32[32,1024]{1,0:T(8,128)S(1)}, f32[32,1024]{1,0:T(8,128)S(1)}, u32[]{:S(2)}, u32[]{:S(2)}) collective-permute-start(f32[32,1024]{1,0:T(8,128)S(1)} %get-tuple-element.33), channel_id=1, source_target_pairs={{0,6},{1,7},{2,4},{3,5},{4,2},{5,3},{6,0},{7,1},{8,14},{9,15},{10,... | collective-permute-start | bytes 393224 | tf_op jit(solution)/shard_map/ppermute | solution.py:174
  8.8 4.3 %collective-permute-start.1 = (f32[8,1024]{1,0:T(8,128)S(1)}, f32[8,1024]{1,0:T(8,128)S(1)}, u32[]{:S(2)}, u32[]{:S(2)}) collective-permute-start(f32[8,1024]{1,0:T(8,128)S(1)} %get-tuple-element.31), channel_id=1, source_target_pairs={{0,16},{1,17},{2,18},{3,19},{4,20},{5,21},{6,22},{7,23},{8,24},{9,... | collective-permute-start | bytes 98312 | tf_op jit(solution)/shard_map/ppermute | solution.py:174
  11.7 9.6 %collective-permute-start = (f32[16,1024]{1,0:T(8,128)S(1)}, f32[16,1024]{1,0:T(8,128)S(1)}, u32[]{:S(2)}, u32[]{:S(2)}) collective-permute-start(f32[16,1024]{1,0:T(8,128)S(1)} %get-tuple-element.30), channel_id=1, source_target_pairs={{0,8},{1,9},{2,10},{3,11},{4,12},{5,13},{6,14},{7,15},{8,0},{9,1},... | collective-permute-start | bytes 196616 | tf_op jit(solution)/shard_map/ppermute | solution.py:174
  13.1 5.4 %collective-permute-start.2 = (f32[8,1024]{1,0:T(8,128)S(1)}, f32[8,1024]{1,0:T(8,128)S(1)}, u32[]{:S(2)}, u32[]{:S(2)}) collective-permute-start(f32[8,1024]{1,0:T(8,128)S(1)} %get-tuple-element.31), channel_id=1, source_target_pairs={{0,24},{1,25},{2,26},{3,27},{4,28},{5,29},{6,30},{7,31},{8,16},{9,... | collective-permute-start | bytes 98312 | tf_op jit(solution)/shard_map/ppermute | solution.py:174
  18.5 7.2 %collective-permute-start.9 = (f32[128,1024]{1,0:T(8,128)S(1)}, f32[128,1024]{1,0:T(8,128)S(1)}, u32[]{:S(2)}, u32[]{:S(2)}) collective-permute-start(f32[128,1024]{1,0:T(8,128)S(1)} %get-tuple-element.40), channel_id=1, source_target_pairs={{0,1},{1,0},{2,3},{3,2},{4,5},{5,4},{6,7},{7,6},{8,9},{9,8},{10,11... | collective-permute-start | bytes 1572872 | tf_op jit(solution)/shard_map/ppermute | solution.py:174
  21.4 5.4 %collective-permute-start.10 = (f32[128,1024]{1,0:T(8,128)S(1)}, f32[128,1024]{1,0:T(8,128)S(1)}, u32[]{:S(2)}, u32[]{:S(2)}) collective-permute-start(f32[128,1024]{1,0:T(8,128)S(1)} %pad_maximum_fusion), channel_id=1, source_target_pairs={{0,1},{1,0},{2,3},{3,2},{4,5},{5,4},{6,7},{7,6},{8,9},{9,8},{10,11... | collective-permute-start | bytes 1572872 | tf_op jit(solution)/shard_map/ppermute | solution.py:174
  21.5 7.3 %collective-permute-start.6 = (f32[32,1024]{1,0:T(8,128)S(1)}, f32[32,1024]{1,0:T(8,128)S(1)}, u32[]{:S(2)}, u32[]{:S(2)}) collective-permute-start(f32[32,1024]{1,0:T(8,128)S(1)} %constant_dynamic-update-slice_fusion.refs_0_), channel_id=1, source_target_pairs={{0,2},{1,3},{2,0},{3,1},{4,6},{5,7},{6,4},{7,5},{8,10},{9,11},{10,... | collective-permute-start | bytes 393224 | tf_op jit(solution)/shard_map/ppermute | solution.py:174
  21.6 10.0 %collective-permute-start.7 = (f32[32,1024]{1,0:T(8,128)S(1)}, f32[32,1024]{1,0:T(8,128)S(1)}, u32[]{:S(2)}, u32[]{:S(2)}) collective-permute-start(f32[32,1024]{1,0:T(8,128)S(1)} %constant_dynamic-update-slice_fusion.refs_0_), channel_id=1, source_target_pairs={{0,4},{1,5},{2,6},{3,7},{4,0},{5,1},{6,2},{7,3},{8,12},{9,13},{10,... | collective-permute-start | bytes 393224 | tf_op jit(solution)/shard_map/ppermute | solution.py:174
  25.7 8.5 %collective-permute-start.8 = (f32[32,1024]{1,0:T(8,128)S(1)}, f32[32,1024]{1,0:T(8,128)S(1)}, u32[]{:S(2)}, u32[]{:S(2)}) collective-permute-start(f32[32,1024]{1,0:T(8,128)S(1)} %constant_dynamic-update-slice_fusion.refs_0_), channel_id=1, source_target_pairs={{0,6},{1,7},{2,4},{3,5},{4,2},{5,3},{6,0},{7,1},{8,14},{9,15},{10,... | collective-permute-start | bytes 393224 | tf_op jit(solution)/shard_map/ppermute | solution.py:174
  25.7 10.0 %collective-permute-start.11 = (f32[32,1024]{1,0:T(8,128)S(1)}, f32[32,1024]{1,0:T(8,128)S(1)}, u32[]{:S(2)}, u32[]{:S(2)}) collective-permute-start(f32[32,1024]{1,0:T(8,128)S(1)} %constant_dynamic-update-slice_fusion.refs_0_), channel_id=1, source_target_pairs={{0,1},{1,0},{2,3},{3,2},{4,5},{5,4},{6,7},{7,6},{8,9},{9,8},{10,11... | collective-permute-start | bytes 393224 | tf_op jit(solution)/shard_map/ppermute | solution.py:174
  26.8 10.0 %copy-start.2 = (bf16[512,512]{1,0:T(8,128)(2,1)S(1)}, bf16[512,512]{1,0:T(8,128)(2,1)}, u32[]{:S(2)}) copy-start(bf16[512,512]{1,0:T(8,128)(2,1)} %refs_12_.1) | copy-start | bytes 1572868
  34.1 2.1 %collective-permute-start.12 = (f32[32,1024]{1,0:T(8,128)S(1)}, f32[32,1024]{1,0:T(8,128)S(1)}, u32[]{:S(2)}, u32[]{:S(2)}) collective-permute-start(f32[32,1024]{1,0:T(8,128)S(1)} %collective-permute-done.6.refs_1_), channel_id=1, source_target_pairs={{0,1},{1,0},{2,3},{3,2},{4,5},{5,4},{6,7},{7,6},{8,9},{9,8},{10,11... | collective-permute-start | bytes 393224 | tf_op jit(solution)/shard_map/ppermute | solution.py:174
  35.2 1.3 %collective-permute-start.13 = (f32[32,1024]{1,0:T(8,128)S(1)}, f32[32,1024]{1,0:T(8,128)S(1)}, u32[]{:S(2)}, u32[]{:S(2)}) collective-permute-start(f32[32,1024]{1,0:T(8,128)S(1)} %collective-permute-done.7.refs_2_), channel_id=1, source_target_pairs={{0,1},{1,0},{2,3},{3,2},{4,5},{5,4},{6,7},{7,6},{8,9},{9,8},{10,11... | collective-permute-start | bytes 393224 | tf_op jit(solution)/shard_map/ppermute | solution.py:174
  35.2 1.5 %collective-permute-start.14 = (f32[32,1024]{1,0:T(8,128)S(1)}, f32[32,1024]{1,0:T(8,128)S(1)}, u32[]{:S(2)}, u32[]{:S(2)}) collective-permute-start(f32[32,1024]{1,0:T(8,128)S(1)} %collective-permute-done.8.refs_3_), channel_id=1, source_target_pairs={{0,1},{1,0},{2,3},{3,2},{4,5},{5,4},{6,7},{7,6},{8,9},{9,8},{10,11... | collective-permute-start | bytes 393224 | tf_op jit(solution)/shard_map/ppermute | solution.py:174

commit v2 on v1

--- a/solution.py
+++ b/solution.py
@@ -16,15 +16,16 @@
 F32 = jnp.float32
 BF16 = jnp.bfloat16
 VMEM = pl.BlockSpec(memory_space=pltpu.VMEM)
+HBM = pl.BlockSpec(memory_space=pltpu.HBM)
 PARAMS = pltpu.CompilerParams(vmem_limit_bytes=48 * 1024 * 1024)
 
 
-def call(body, outs, *args, scratch=(), place=VMEM):
+def call(body, outs, *args, scratch=(), place=VMEM, out_place=VMEM):
     return pl.pallas_call(
         body,
         out_shape=outs,
         in_specs=[place] * len(args),
-        out_specs=jax.tree.map(lambda _: VMEM, outs),
+        out_specs=jax.tree.map(lambda _: out_place, outs),
         scratch_shapes=list(scratch),
         compiler_params=PARAMS,
     )(*args)
@@ -34,10 +35,15 @@
     return jax.ShapeDtypeStruct(dims, dtype)
 
 
-def pool_matrix(rows, cols, level):
-    row = lax.broadcasted_iota(jnp.int32, (rows, cols), 0)
-    col = lax.broadcasted_iota(jnp.int32, (rows, cols), 1)
-    return jnp.where((col >> level) == row, 2.0**-level, 0.0).astype(BF16)
+def pool_matrix(cols, levels, padded):
+    row = lax.broadcasted_iota(jnp.int32, (padded, cols), 0)
+    col = lax.broadcasted_iota(jnp.int32, (padded, cols), 1)
+    pool = jnp.zeros((padded, cols), F32)
+    first = 0
+    for level in levels:
+        pool = jnp.where((col >> level) == row - first, 2.0**-level, pool)
+        first += cols >> level
+    return pool.astype(BF16)
 
 
 def project_kernel(x_hbm, wk_hbm, wv_hbm, k_ref, v_ref, *refs):
@@ -48,18 +54,19 @@
     ]
     for copy in copies:
         copy.start()
+    rows = x_ref.shape[0]
+    pool = pool_matrix(rows, range(2, 7), rows // 2)
     copies[0].wait()
-    for copy, w_ref, r_ref in ((copies[1], wk_ref, k_ref), (copies[2], wv_ref, v_ref)):
-        copy.wait()
-        r_ref[...] = jnp.dot(x_ref[...], w_ref[...], preferred_element_type=F32).astype(BF16)
-    rows = x_ref.shape[0]
-    levels = [2, 3, 4, 5, 6]
-    for level, ref in zip(levels, coarse_refs):
-        pool = pool_matrix(rows >> level, rows, level)
-        for half, r_ref in enumerate((k_ref, v_ref)):
-            ref[:, half * D : (half + 1) * D] = jnp.dot(
-                pool, r_ref[...], preferred_element_type=F32
-            )
+    for half, w_ref, r_ref in ((0, wk_ref, k_ref), (1, wv_ref, v_ref)):
+        copies[1 + half].wait()
+        fine = jnp.dot(x_ref[...], w_ref[...], preferred_element_type=F32).astype(BF16)
+        r_ref[...] = fine
+        pooled = jnp.dot(pool, fine, preferred_element_type=F32)
+        first = 0
+        for ref in coarse_refs:
+            n = ref.shape[0]
+            ref[:, half * D : (half + 1) * D] = pooled[first : first + n]
+            first += n
 
 
 def term(keys, query, value_t):
@@ -79,7 +86,11 @@
     return common, denom, numer
 
 
-def local_kernel(x_ref, wq_ref, k_ref, v_ref, q_ref, top_ref, den_ref, acc_ref, vt_ref, k1_ref, v1t_ref):
+def local_kernel(x_ref, wq_ref, k_ref, v_ref, s2_ref, z1_ref, near_ref, q_ref, top_ref, den_ref, acc_ref, *scratch):
+    vt_ref, k1_ref, v1t_ref, kc_ref, vct_ref = scratch
+    half = BLK // 2
+    plan = [[(0, 0, BLK)], [(1, 0, half), (2, 0, half)]]
+    stage([s2_ref, z1_ref, near_ref], plan, kc_ref, vct_ref)
     rows = x_ref.shape[0]
     q = jnp.dot(x_ref[...], wq_ref[...], preferred_element_type=F32).astype(BF16)
     qt = (q.astype(F32) * 0.125).T
@@ -88,7 +99,7 @@
     q_ref[0] = jnp.where(even, qt, 0.0).astype(BF16)
     q_ref[1] = jnp.where(even, 0.0, qt).astype(BF16)
     vt_ref[...] = v_ref[...].astype(F32).T.astype(BF16)
-    pool = pool_matrix(rows // 2, rows, 1)
+    pool = pool_matrix(rows, (1,), rows // 2)
     k1_ref[...] = jnp.dot(pool, k_ref[...], preferred_element_type=F32).astype(BF16)
     v1 = jnp.dot(pool, v_ref[...], preferred_element_type=F32)
     v1t_ref[...] = v1.T.astype(BF16)
@@ -106,6 +117,7 @@
             span = slice(far * BLK, (far + 1) * BLK)
             top, denom, numer = term(k1_ref[span, pair], query, v1t_ref[own, span])
             parts.append((top + LN2, denom, numer))
+            parts += remote_terms(head, cols, q_ref, kc_ref, vct_ref, (2, 3))
             top, denom, numer = merge(parts)
             top_ref[head : head + 1, cols] = top
             den_ref[head : head + 1, cols] = denom
@@ -139,17 +151,6 @@
     for head in range(HEADS):
         for lo in range(0, rows, BLK):
             yield head, slice(head * HEAD_DIM, (head + 1) * HEAD_DIM), slice(lo, lo + BLK)
-
-
-def middle_kernel(plan, levels, n, *refs):
-    rows, (q_ref, top_in, den_in, acc_in) = refs[:n], refs[n : n + 4]
-    top_ref, den_ref, acc_ref, kc_ref, vct_ref = refs[n + 4 :]
-    stage(rows, plan, kc_ref, vct_ref)
-    for head, own, cols in chunks(acc_ref.shape[1]):
-        parts = remote_terms(head, cols, q_ref, kc_ref, vct_ref, levels)
-        one = slice(head, head + 1)
-        parts.append((top_in[one, cols], den_in[one, cols], acc_in[own, cols]))
-        top_ref[one, cols], den_ref[one, cols], acc_ref[own, cols] = merge(parts)
 
 
 def final_kernel(plan, levels, n, *refs):
@@ -180,11 +181,17 @@
         scratch=[pltpu.VMEM((rows, D), BF16)]
         + [pltpu.VMEM((D, D), BF16)] * 2
         + [pltpu.SemaphoreType.DMA((3,))],
-        place=pl.BlockSpec(memory_space=pltpu.HBM),
-    )
+        place=HBM,
+    )
+    z1, z3 = swap(c3, 2), swap(c4, 6)
     y1, y2, y3 = swap(c5, 8), swap(c6, 16), swap(c6, 24)
+    y1, y2, y3, z1 = lax.optimization_barrier((y1, y2, y3, z1))
+    g = jnp.concatenate([y1, y2, y3], axis=0)
+    near = swap(z1, 1)
     s2 = swap(c2, 1)
-    z1, z2, z3 = swap(c3, 2), swap(c4, 4), swap(c4, 6)
+    f0 = swap(g, 1)
+    g2 = swap(jnp.concatenate([g, c4], axis=0), 4)
+    g1, g3 = swap(g, 2), swap(g, 6)
     state = [shape(HEADS, rows), shape(HEADS, rows), shape(D, rows)]
     q, top, den, acc = call(
         local_kernel,
@@ -193,38 +200,28 @@
         w_query,
         k,
         v,
+        s2,
+        z1,
+        near,
         scratch=[
             pltpu.VMEM((D, rows), BF16),
             pltpu.VMEM((rows // 2, D), BF16),
             pltpu.VMEM((D, rows // 2), BF16),
+            pltpu.VMEM((2, BLK, D), BF16),
+            pltpu.VMEM((2, D, BLK), BF16),
         ],
     )
-    y1, y2, y3, z1, z2, z3, top = lax.optimization_barrier((y1, y2, y3, z1, z2, z3, top))
-    g = jnp.concatenate([y1, y2, y3], axis=0)
-    g1, g2, g3 = swap(g, 2), swap(g, 4), swap(g, 6)
-    near = swap(jnp.concatenate([z1, z2, z3], axis=0), 1)
+    z3, g1, g2, g3, top = lax.optimization_barrier((z3, g1, g2, g3, top))
+    zf = swap(z3, 1)
     def staged(slots):
         return [pltpu.VMEM((slots, BLK, D), BF16), pltpu.VMEM((slots, D, BLK), BF16)]
 
-    arrays = [s2, z1, z2, z3, near]
-    plan = [[(0, 0, 128)], [(1, 0, 64), (4, 0, 64)], [(2, 0, 32), (3, 0, 32), (4, 64, 64)]]
-    top, den, acc = call(
-        functools.partial(middle_kernel, plan, (2, 3, 4), len(arrays)),
-        state,
-        *arrays,
-        q,
-        top,
-        den,
-        acc,
-        scratch=staged(3),
-    )
-    f0 = swap(g, 1)
-    g1, g2, g3, top = lax.optimization_barrier((g1, g2, g3, top))
-    f1, f2, f3 = [swap(part, 1) for part in (g1, g2, g3)]
-    arrays = [g, g1, g2, g3, f0, f1, f2, f3]
-    plan = [[(i, lo, 16) for i in range(8)] for lo in (0, 16)]
+    f1, f2, f3 = swap(g1, 1), swap(g2, 1), swap(g3, 1)
+    arrays = [g, f0, g1, f1, g2, f2, g3, f3, z3, zf]
+    plan = [[(i, at, 16) for i in range(8)] for at in (0, 16)]
+    plan = [[(4, 32, 32), (5, 32, 32), (8, 0, 32), (9, 0, 32)]] + plan
     return call(
-        functools.partial(final_kernel, plan, (5, 6), len(arrays)),
+        functools.partial(final_kernel, plan, (4, 5, 6), len(arrays)),
         shape(rows, D, dtype=BF16),
         *arrays,
         q,
@@ -232,7 +229,7 @@
         den,
         acc,
         w_output,
-        scratch=staged(2) + [pltpu.VMEM((D, rows), F32)],
+        scratch=staged(3) + [pltpu.VMEM((D, rows), F32)],
     )
 
 

time: 39.5 us -> 34.5 us (0.87)
  starting transfers between devices: 21.7 us -> 18.1 us
  waiting for transfers between devices: 7.32 us -> 6.65 us
  Pallas kernels: 10.2 us -> 9.55 us
    ppermute x15, starting transfers between devices: 21.7 us -> 18.1 us  [swap(): return lax.ppermute(block, 'seq', [(i, i ^ apart) for i in range(count)])]
    ppermute x15, waiting for transfers between devices: 7.32 us -> 6.65 us  [swap(): return lax.ppermute(block, 'seq', [(i, i ^ apart) for i in range(count)])]
    pallas_call x4 -> x3, Pallas kernels: 10.2 us -> 9.55 us  [call(): pl.pallas_call(body, out_shape=outs, in_specs=[place] * len(args), out_sp...]
  transfers between devices with their start and end apart: 15 -> 15, of which waited for: 6 -> 7; matrix products, arithmetic and copies ran while one was open for 0% -> 0% of each run, Pallas kernels for 12% -> 11%
where the time goes in v2:
time: 34.5 us; the launch traced here: 34.4 us
  starting transfers between devices  18.1 us (52%)
  Pallas kernels  9.55 us (28%)
  waiting for transfers between devices  6.65 us (19%)
    ppermute x15, starting transfers between devices, swap(): return lax.ppermute(block, 'seq', [(i, i ^ apart) for i in range(count)])  18.1 us
    pallas_call x3, Pallas kernels, call(): pl.pallas_call(body, out_shape=outs, in_specs=[place] * len(args), out_sp...  9.55 us
    ppermute x15, waiting for transfers between devices, swap(): return lax.ppermute(block, 'seq', [(i, i ^ apart) for i in range(count)])  6.65 us
  transfers between devices with their start and end apart: 15, of which 7 were waited for; matrix products, arithmetic and copies ran while one was open for 0% of the time, Pallas kernels for 11%

profile of v2, /device:TPU:1, one launch (start us, length us, event | category | flops | bytes accessed | tf_op | source)
XLA Modules:
  0.0 34.4 jit_solution(12964061007311327025)
XLA Ops:
  0.0 2.6 %shard_map.55 = (bf16[512,512]{1,0:T(8,128)(2,1)S(1)}, bf16[512,512]{1,0:T(8,128)(2,1)S(1)}, f32[128,1024]{1,0:T(8,128)S(1)}, f32[64,1024]{1,0:T(8,128)S(1)}, f3...) custom-call(bf16[512,512]{1,0:T(8,128)(2,1)} %x_ref.1, bf16[512,512]{1,0:T(8,128)(2,1)} %wk_hbm.1, ...), custom_call_target="tpu_custom_call" | custom-call | tf_op jit(solution)/shard_map/pallas_call | solution.py:24
  2.6 0.0 copy-start
  2.6 2.5 %collective-permute-start.3 = (f32[64,1024]{1,0:T(8,128)S(1)}, f32[64,1024]{1,0:T(8,128)S(1)}, u32[]{:S(2)}, u32[]{:S(2)}) collective-permute-start(f32[64,1024]{1,0:T(8,128)S(1)} %get-tuple-element.27), channel_id=1, source_target_pairs={{0,2},{1,3},{2,0},{3,1},{4,6},{5,7},{6,4},{7,5},{8,10},{9,11},{10,... | collective-permute-start | bytes 786440 | tf_op jit(solution)/shard_map/ppermute | solution.py:175
  5.1 1.3 %collective-permute-start = (f32[16,1024]{1,0:T(8,128)S(1)}, f32[16,1024]{1,0:T(8,128)S(1)}, u32[]{:S(2)}, u32[]{:S(2)}) collective-permute-start(f32[16,1024]{1,0:T(8,128)S(1)} %get-tuple-element.25), channel_id=1, source_target_pairs={{0,8},{1,9},{2,10},{3,11},{4,12},{5,13},{6,14},{7,15},{8,0},{9,1},... | collective-permute-start | bytes 196616 | tf_op jit(solution)/shard_map/ppermute | solution.py:175
  6.4 2.6 %collective-permute-start.1 = (f32[8,1024]{1,0:T(8,128)S(1)}, f32[8,1024]{1,0:T(8,128)S(1)}, u32[]{:S(2)}, u32[]{:S(2)}) collective-permute-start(f32[8,1024]{1,0:T(8,128)S(1)} %get-tuple-element.26), channel_id=1, source_target_pairs={{0,16},{1,17},{2,18},{3,19},{4,20},{5,21},{6,22},{7,23},{8,24},{9,... | collective-permute-start | bytes 98312 | tf_op jit(solution)/shard_map/ppermute | solution.py:175
  9.1 0.0 collective-permute-start.2
  9.1 1.7 %collective-permute-start.9 = (f32[128,1024]{1,0:T(8,128)S(1)}, f32[128,1024]{1,0:T(8,128)S(1)}, u32[]{:S(2)}, u32[]{:S(2)}) collective-permute-start(f32[128,1024]{1,0:T(8,128)S(1)} %get-tuple-element.34), channel_id=1, source_target_pairs={{0,1},{1,0},{2,3},{3,2},{4,5},{5,4},{6,7},{7,6},{8,9},{9,8},{10,11... | collective-permute-start | bytes 1572872 | tf_op jit(solution)/shard_map/ppermute | solution.py:175
  10.8 0.3 collective-permute-done.1
  11.1 2.2 %collective-permute-start.5 = (f32[32,1024]{1,0:T(8,128)S(1)}, f32[32,1024]{1,0:T(8,128)S(1)}, u32[]{:S(2)}, u32[]{:S(2)}) collective-permute-start(f32[32,1024]{1,0:T(8,128)S(1)} %get-tuple-element.31), channel_id=1, source_target_pairs={{0,6},{1,7},{2,4},{3,5},{4,2},{5,3},{6,0},{7,1},{8,14},{9,15},{10,... | collective-permute-start | bytes 393224 | tf_op jit(solution)/shard_map/ppermute | solution.py:175
  13.3 0.0 collective-permute-done.2
  13.3 2.5 %collective-permute-start.10 = (f32[64,1024]{1,0:T(8,128)S(1)}, f32[64,1024]{1,0:T(8,128)S(1)}, u32[]{:S(2)}, u32[]{:S(2)}) collective-permute-start(f32[64,1024]{1,0:T(8,128)S(1)} %collective-permute-done.3.z1_ref), channel_id=1, source_target_pairs={{0,1},{1,0},{2,3},{3,2},{4,5},{5,4},{6,7},{7,6},{8,9},{9,8},{10,11... | collective-permute-start | bytes 786440 | tf_op jit(solution)/shard_map/ppermute | solution.py:175
  15.8 3.3 %collective-permute-start.7 = (f32[64,1024]{1,0:T(8,128)S(1)}, f32[64,1024]{1,0:T(8,128)S(1)}, u32[]{:S(2)}, u32[]{:S(2)}) collective-permute-start(f32[64,1024]{1,0:T(8,128)S(1)} %pad_maximum_fusion), channel_id=1, source_target_pairs={{0,4},{1,5},{2,6},{3,7},{4,0},{5,1},{6,2},{7,3},{8,12},{9,13},{10,... | collective-permute-start | bytes 786440 | tf_op jit(solution)/shard_map/ppermute | solution.py:175
  19.1 0.1 collective-permute-start.6
  19.2 0.3 collective-permute-start.8
  19.5 0.0 collective-permute-done.9.s2_ref
  19.5 0.0 copy-start.1
  19.6 3.8 %shard_map.56 = (bf16[2,512,512]{2,1,0:T(8,128)(2,1)S(1)}, f32[8,512]{1,0:T(8,128)S(1)}, f32[8,512]{1,0:T(8,128)S(1)}, f32[512,512]{1,0:T(8,128)S(1)}) custom-call(bf16[512,512]{1,0:T(8,128)(2,1)S(1)} %copy-done, bf16[512,512]{1,0:T(8,128)(2,1)S(1)} %copy-done.2, bf16[512,512]{1,0:T(8,128)(2,1)S(1)} %get-tuple-element.32.k_ref, ...), custom_call_target="tpu_custom_call" | custom-call | tf_op jit(solution)/shard_map/pallas_call | solution.py:24
  23.4 0.0 collective-permute-done.5.refs_8_
  23.4 4.6 %collective-permute-done.6.refs_2_ = f32[32,1024]{1,0:T(8,128)S(1)} collective-permute-done((f32[32,1024]{1,0:T(8,128)S(1)}, f32[32,1024]{1,0:T(8,128)S(1)}, u32[]{:S(2)}, u32[]{:S(2)}) %collective-permute-start.6) | collective-permute-done | bytes 131104 | tf_op jit(solution)/shard_map/ppermute | solution.py:175
  28.0 0.8 %collective-permute-done.8.refs_6_ = f32[32,1024]{1,0:T(8,128)S(1)} collective-permute-done((f32[32,1024]{1,0:T(8,128)S(1)}, f32[32,1024]{1,0:T(8,128)S(1)}, u32[]{:S(2)}, u32[]{:S(2)}) %collective-permute-start.8) | collective-permute-done | bytes 131104 | tf_op jit(solution)/shard_map/ppermute | solution.py:175
  28.7 0.0 collective-permute-done.7.refs_4_
  28.7 0.5 %collective-permute-start.12 = (f32[64,1024]{1,0:T(8,128)S(1)}, f32[64,1024]{1,0:T(8,128)S(1)}, u32[]{:S(2)}, u32[]{:S(2)}) collective-permute-start(f32[64,1024]{1,0:T(8,128)S(1)} %collective-permute-done.7.refs_4_), channel_id=1, source_target_pairs={{0,1},{1,0},{2,3},{3,2},{4,5},{5,4},{6,7},{7,6},{8,9},{9,8},{10,11... | collective-permute-start | bytes 786440 | tf_op jit(solution)/shard_map/ppermute | solution.py:175
  29.2 0.0 collective-permute-start.4
  29.2 0.5 %collective-permute-start.11 = (f32[32,1024]{1,0:T(8,128)S(1)}, f32[32,1024]{1,0:T(8,128)S(1)}, u32[]{:S(2)}, u32[]{:S(2)}) collective-permute-start(f32[32,1024]{1,0:T(8,128)S(1)} %collective-permute-done.6.refs_2_), channel_id=1, source_target_pairs={{0,1},{1,0},{2,3},{3,2},{4,5},{5,4},{6,7},{7,6},{8,9},{9,8},{10,11... | collective-permute-start | bytes 393224 | tf_op jit(solution)/shard_map/ppermute | solution.py:175
  29.7 0.0 collective-permute-start.13
  29.8 0.5 %collective-permute-start.14 = (f32[32,1024]{1,0:T(8,128)S(1)}, f32[32,1024]{1,0:T(8,128)S(1)}, u32[]{:S(2)}, u32[]{:S(2)}) collective-permute-start(f32[32,1024]{1,0:T(8,128)S(1)} %collective-permute-done.5.refs_8_), channel_id=1, source_target_pairs={{0,1},{1,0},{2,3},{3,2},{4,5},{5,4},{6,7},{7,6},{8,9},{9,8},{10,11... | collective-permute-start | bytes 393224 | tf_op jit(solution)/shard_map/ppermute | solution.py:175
  30.2 0.3 collective-permute-done.4.refs_1_
  30.6 0.2 collective-permute-done.11.refs_3_
  30.7 0.3 collective-permute-done.13.refs_7_
  31.1 0.2 collective-permute-done.14.refs_9_
  31.2 0.0 collective-permute-done.12.refs_5_
  31.3 3.2 %shard_map.57 = bf16[512,512]{1,0:T(8,128)(2,1)} custom-call(f32[32,1024]{1,0:T(8,128)S(1)} %constant_dynamic-update-slice_fusion.refs_0_, f32[32,1024]{1,0:T(8,128)S(1)} %collective-permute-done.4.refs_1_, f32[32,1024]{1,0:T(8,128)S(1)} %collective-permute-done.6.refs_2_, f32[32,1024]{1,0:T(8,128)S(1)} %collective-permute-done.11.refs_3_, ...), custom_call_target="tpu_custom_call" | custom-call | tf_op jit(solution)/shard_map/pallas_call | solution.py:24
  (11 shorter events, 0.0 us)
Async XLA Ops:
  0.0 19.5 %copy-start.2 = (bf16[512,512]{1,0:T(8,128)(2,1)S(1)}, bf16[512,512]{1,0:T(8,128)(2,1)}, u32[]{:S(2)}) copy-start(bf16[512,512]{1,0:T(8,128)(2,1)} %wq_ref.1) | copy-start | bytes 1572868
  2.6 17.0 %copy-start = (bf16[512,512]{1,0:T(8,128)(2,1)S(1)}, bf16[512,512]{1,0:T(8,128)(2,1)}, u32[]{:S(2)}) copy-start(bf16[512,512]{1,0:T(8,128)(2,1)} %x_ref.1) | copy-start | bytes 1572868
  2.6 10.7 %collective-permute-start.3 = (f32[64,1024]{1,0:T(8,128)S(1)}, f32[64,1024]{1,0:T(8,128)S(1)}, u32[]{:S(2)}, u32[]{:S(2)}) collective-permute-start(f32[64,1024]{1,0:T(8,128)S(1)} %get-tuple-element.27), channel_id=1, source_target_pairs={{0,2},{1,3},{2,0},{3,1},{4,6},{5,7},{6,4},{7,5},{8,10},{9,11},{10,... | collective-permute-start | bytes 786440 | tf_op jit(solution)/shard_map/ppermute | solution.py:175
  5.1 8.2 %collective-permute-start = (f32[16,1024]{1,0:T(8,128)S(1)}, f32[16,1024]{1,0:T(8,128)S(1)}, u32[]{:S(2)}, u32[]{:S(2)}) collective-permute-start(f32[16,1024]{1,0:T(8,128)S(1)} %get-tuple-element.25), channel_id=1, source_target_pairs={{0,8},{1,9},{2,10},{3,11},{4,12},{5,13},{6,14},{7,15},{8,0},{9,1},... | collective-permute-start | bytes 196616 | tf_op jit(solution)/shard_map/ppermute | solution.py:175
  6.4 4.6 %collective-permute-start.1 = (f32[8,1024]{1,0:T(8,128)S(1)}, f32[8,1024]{1,0:T(8,128)S(1)}, u32[]{:S(2)}, u32[]{:S(2)}) collective-permute-start(f32[8,1024]{1,0:T(8,128)S(1)} %get-tuple-element.26), channel_id=1, source_target_pairs={{0,16},{1,17},{2,18},{3,19},{4,20},{5,21},{6,22},{7,23},{8,24},{9,... | collective-permute-start | bytes 98312 | tf_op jit(solution)/shard_map/ppermute | solution.py:175
  9.1 4.3 %collective-permute-start.2 = (f32[8,1024]{1,0:T(8,128)S(1)}, f32[8,1024]{1,0:T(8,128)S(1)}, u32[]{:S(2)}, u32[]{:S(2)}) collective-permute-start(f32[8,1024]{1,0:T(8,128)S(1)} %get-tuple-element.26), channel_id=1, source_target_pairs={{0,24},{1,25},{2,26},{3,27},{4,28},{5,29},{6,30},{7,31},{8,16},{9,... | collective-permute-start | bytes 98312 | tf_op jit(solution)/shard_map/ppermute | solution.py:175
  9.1 10.5 %collective-permute-start.9 = (f32[128,1024]{1,0:T(8,128)S(1)}, f32[128,1024]{1,0:T(8,128)S(1)}, u32[]{:S(2)}, u32[]{:S(2)}) collective-permute-start(f32[128,1024]{1,0:T(8,128)S(1)} %get-tuple-element.34), channel_id=1, source_target_pairs={{0,1},{1,0},{2,3},{3,2},{4,5},{5,4},{6,7},{7,6},{8,9},{9,8},{10,11... | collective-permute-start | bytes 1572872 | tf_op jit(solution)/shard_map/ppermute | solution.py:175
  11.1 12.3 %collective-permute-start.5 = (f32[32,1024]{1,0:T(8,128)S(1)}, f32[32,1024]{1,0:T(8,128)S(1)}, u32[]{:S(2)}, u32[]{:S(2)}) collective-permute-start(f32[32,1024]{1,0:T(8,128)S(1)} %get-tuple-element.31), channel_id=1, source_target_pairs={{0,6},{1,7},{2,4},{3,5},{4,2},{5,3},{6,0},{7,1},{8,14},{9,15},{10,... | collective-permute-start | bytes 393224 | tf_op jit(solution)/shard_map/ppermute | solution.py:175
  13.3 5.9 %collective-permute-start.10 = (f32[64,1024]{1,0:T(8,128)S(1)}, f32[64,1024]{1,0:T(8,128)S(1)}, u32[]{:S(2)}, u32[]{:S(2)}) collective-permute-start(f32[64,1024]{1,0:T(8,128)S(1)} %collective-permute-done.3.z1_ref), channel_id=1, source_target_pairs={{0,1},{1,0},{2,3},{3,2},{4,5},{5,4},{6,7},{7,6},{8,9},{9,8},{10,11... | collective-permute-start | bytes 786440 | tf_op jit(solution)/shard_map/ppermute | solution.py:175
  15.8 12.9 %collective-permute-start.7 = (f32[64,1024]{1,0:T(8,128)S(1)}, f32[64,1024]{1,0:T(8,128)S(1)}, u32[]{:S(2)}, u32[]{:S(2)}) collective-permute-start(f32[64,1024]{1,0:T(8,128)S(1)} %pad_maximum_fusion), channel_id=1, source_target_pairs={{0,4},{1,5},{2,6},{3,7},{4,0},{5,1},{6,2},{7,3},{8,12},{9,13},{10,... | collective-permute-start | bytes 786440 | tf_op jit(solution)/shard_map/ppermute | solution.py:175
  19.1 8.8 %collective-permute-start.6 = (f32[32,1024]{1,0:T(8,128)S(1)}, f32[32,1024]{1,0:T(8,128)S(1)}, u32[]{:S(2)}, u32[]{:S(2)}) collective-permute-start(f32[32,1024]{1,0:T(8,128)S(1)} %constant_dynamic-update-slice_fusion.refs_0_), channel_id=1, source_target_pairs={{0,2},{1,3},{2,0},{3,1},{4,6},{5,7},{6,4},{7,5},{8,10},{9,11},{10,... | collective-permute-start | bytes 393224 | tf_op jit(solution)/shard_map/ppermute | solution.py:175
  19.2 9.5 %collective-permute-start.8 = (f32[32,1024]{1,0:T(8,128)S(1)}, f32[32,1024]{1,0:T(8,128)S(1)}, u32[]{:S(2)}, u32[]{:S(2)}) collective-permute-start(f32[32,1024]{1,0:T(8,128)S(1)} %constant_dynamic-update-slice_fusion.refs_0_), channel_id=1, source_target_pairs={{0,6},{1,7},{2,4},{3,5},{4,2},{5,3},{6,0},{7,1},{8,14},{9,15},{10,... | collective-permute-start | bytes 393224 | tf_op jit(solution)/shard_map/ppermute | solution.py:175
  19.5 11.7 %copy-start.1 = (bf16[512,512]{1,0:T(8,128)(2,1)S(1)}, bf16[512,512]{1,0:T(8,128)(2,1)}, u32[]{:S(2)}) copy-start(bf16[512,512]{1,0:T(8,128)(2,1)} %refs_14_.1) | copy-start | bytes 1572868
  28.7 2.5 %collective-permute-start.12 = (f32[64,1024]{1,0:T(8,128)S(1)}, f32[64,1024]{1,0:T(8,128)S(1)}, u32[]{:S(2)}, u32[]{:S(2)}) collective-permute-start(f32[64,1024]{1,0:T(8,128)S(1)} %collective-permute-done.7.refs_4_), channel_id=1, source_target_pairs={{0,1},{1,0},{2,3},{3,2},{4,5},{5,4},{6,7},{7,6},{8,9},{9,8},{10,11... | collective-permute-start | bytes 786440 | tf_op jit(solution)/shard_map/ppermute | solution.py:175
  29.2 1.3 %collective-permute-start.4 = (f32[32,1024]{1,0:T(8,128)S(1)}, f32[32,1024]{1,0:T(8,128)S(1)}, u32[]{:S(2)}, u32[]{:S(2)}) collective-permute-start(f32[32,1024]{1,0:T(8,128)S(1)} %constant_dynamic-update-slice_fusion.refs_0_), channel_id=1, source_target_pairs={{0,1},{1,0},{2,3},{3,2},{4,5},{5,4},{6,7},{7,6},{8,9},{9,8},{10,11... | collective-permute-start | bytes 393224 | tf_op jit(solution)/shard_map/ppermute | solution.py:175
  29.2 1.5 %collective-permute-start.11 = (f32[32,1024]{1,0:T(8,128)S(1)}, f32[32,1024]{1,0:T(8,128)S(1)}, u32[]{:S(2)}, u32[]{:S(2)}) collective-permute-start(f32[32,1024]{1,0:T(8,128)S(1)} %collective-permute-done.6.refs_2_), channel_id=1, source_target_pairs={{0,1},{1,0},{2,3},{3,2},{4,5},{5,4},{6,7},{7,6},{8,9},{9,8},{10,11... | collective-permute-start | bytes 393224 | tf_op jit(solution)/shard_map/ppermute | solution.py:175
  29.7 1.3 %collective-permute-start.13 = (f32[32,1024]{1,0:T(8,128)S(1)}, f32[32,1024]{1,0:T(8,128)S(1)}, u32[]{:S(2)}, u32[]{:S(2)}) collective-permute-start(f32[32,1024]{1,0:T(8,128)S(1)} %collective-permute-done.8.refs_6_), channel_id=1, source_target_pairs={{0,1},{1,0},{2,3},{3,2},{4,5},{5,4},{6,7},{7,6},{8,9},{9,8},{10,11... | collective-permute-start | bytes 393224 | tf_op jit(solution)/shard_map/ppermute | solution.py:175
  29.8 1.5 %collective-permute-start.14 = (f32[32,1024]{1,0:T(8,128)S(1)}, f32[32,1024]{1,0:T(8,128)S(1)}, u32[]{:S(2)}, u32[]{:S(2)}) collective-permute-start(f32[32,1024]{1,0:T(8,128)S(1)} %collective-permute-done.5.refs_8_), channel_id=1, source_target_pairs={{0,1},{1,0},{2,3},{3,2},{4,5},{5,4},{6,7},{7,6},{8,9},{9,8},{10,11... | collective-permute-start | bytes 393224 | tf_op jit(solution)/shard_map/ppermute | solution.py:175

commit v3 on v2

--- a/solution.py
+++ b/solution.py
@@ -162,7 +162,7 @@
         one = slice(head, head + 1)
         parts.append((top_in[one, cols], den_in[one, cols], acc_in[own, cols]))
         _, denom, numer = merge(parts)
-        att_ref[own, cols] = numer / denom
+        att_ref[own, cols] = numer * (1.0 / denom)
     att = att_ref[...].T.astype(BF16)
     out_ref[...] = jnp.dot(att, wo_ref[...], preferred_element_type=F32).astype(BF16)
 
@@ -187,9 +187,8 @@
     y1, y2, y3 = swap(c5, 8), swap(c6, 16), swap(c6, 24)
     y1, y2, y3, z1 = lax.optimization_barrier((y1, y2, y3, z1))
     g = jnp.concatenate([y1, y2, y3], axis=0)
-    near = swap(z1, 1)
+    near = swap(jnp.concatenate([z1, g], axis=0), 1)
     s2 = swap(c2, 1)
-    f0 = swap(g, 1)
     g2 = swap(jnp.concatenate([g, c4], axis=0), 4)
     g1, g3 = swap(g, 2), swap(g, 6)
     state = [shape(HEADS, rows), shape(HEADS, rows), shape(D, rows)]
@@ -217,8 +216,10 @@
         return [pltpu.VMEM((slots, BLK, D), BF16), pltpu.VMEM((slots, D, BLK), BF16)]
 
     f1, f2, f3 = swap(g1, 1), swap(g2, 1), swap(g3, 1)
-    arrays = [g, f0, g1, f1, g2, f2, g3, f3, z3, zf]
-    plan = [[(i, at, 16) for i in range(8)] for at in (0, 16)]
+    arrays = [g, near, g1, f1, g2, f2, g3, f3, z3, zf]
+    plan = [
+        [(i, at + (64 if i == 1 else 0), 16) for i in range(8)] for at in (0, 16)
+    ]
     plan = [[(4, 32, 32), (5, 32, 32), (8, 0, 32), (9, 0, 32)]] + plan
     return call(
         functools.partial(final_kernel, plan, (4, 5, 6), len(arrays)),

time: 34.5 us -> 34.4 us (level)
  starting transfers between devices: 18.1 us -> 17.7 us
    ppermute x15 -> x14, starting transfers between devices: 18.1 us -> 17.7 us  [swap(): return lax.ppermute(block, 'seq', [(i, i ^ apart) for i in range(count)])]
    ppermute x15 -> x14, waiting for transfers between devices: 6.65 us -> 6.91 us  [swap(): return lax.ppermute(block, 'seq', [(i, i ^ apart) for i in range(count)])]
  transfers between devices with their start and end apart: 15 -> 14, of which waited for: 7 -> 6; matrix products, arithmetic and copies ran while one was open for 0% -> 0% of each run, Pallas kernels for 11% -> 11%
where the time goes in v3:
time: 34.4 us; the launch traced here: 34.3 us
  starting transfers between devices  17.7 us (51%)
  Pallas kernels  9.5 us (28%)
  waiting for transfers between devices  6.91 us (20%)
    ppermute x14, starting transfers between devices, swap(): return lax.ppermute(block, 'seq', [(i, i ^ apart) for i in range(count)])  17.7 us
    pallas_call x3, Pallas kernels, call(): pl.pallas_call(body, out_shape=outs, in_specs=[place] * len(args), out_sp...  9.5 us
    ppermute x14, waiting for transfers between devices, swap(): return lax.ppermute(block, 'seq', [(i, i ^ apart) for i in range(count)])  6.91 us
  transfers between devices with their start and end apart: 14, of which 6 were waited for; matrix products, arithmetic and copies ran while one was open for 0% of the time, Pallas kernels for 11%

profile of v3, /device:TPU:1, one launch (start us, length us, event | category | flops | bytes accessed | tf_op | source)
XLA Modules:
  0.0 34.3 jit_solution(15422687930487856202)
XLA Ops:
  0.0 2.5 %shard_map.55 = (bf16[512,512]{1,0:T(8,128)(2,1)S(1)}, bf16[512,512]{1,0:T(8,128)(2,1)S(1)}, f32[128,1024]{1,0:T(8,128)S(1)}, f32[64,1024]{1,0:T(8,128)S(1)}, f3...) custom-call(bf16[512,512]{1,0:T(8,128)(2,1)} %x_ref.1, bf16[512,512]{1,0:T(8,128)(2,1)} %wk_hbm.1, ...), custom_call_target="tpu_custom_call" | custom-call | tf_op jit(solution)/shard_map/pallas_call | solution.py:24
  2.5 2.5 %collective-permute-start.3 = (f32[64,1024]{1,0:T(8,128)S(1)}, f32[64,1024]{1,0:T(8,128)S(1)}, u32[]{:S(2)}, u32[]{:S(2)}) collective-permute-start(f32[64,1024]{1,0:T(8,128)S(1)} %get-tuple-element.27), channel_id=1, source_target_pairs={{0,2},{1,3},{2,0},{3,1},{4,6},{5,7},{6,4},{7,5},{8,10},{9,11},{10,... | collective-permute-start | bytes 786440 | tf_op jit(solution)/shard_map/ppermute | solution.py:175
  5.1 1.3 %collective-permute-start = (f32[16,1024]{1,0:T(8,128)S(1)}, f32[16,1024]{1,0:T(8,128)S(1)}, u32[]{:S(2)}, u32[]{:S(2)}) collective-permute-start(f32[16,1024]{1,0:T(8,128)S(1)} %get-tuple-element.25), channel_id=1, source_target_pairs={{0,8},{1,9},{2,10},{3,11},{4,12},{5,13},{6,14},{7,15},{8,0},{9,1},... | collective-permute-start | bytes 196616 | tf_op jit(solution)/shard_map/ppermute | solution.py:175
  6.4 2.6 %collective-permute-start.1 = (f32[8,1024]{1,0:T(8,128)S(1)}, f32[8,1024]{1,0:T(8,128)S(1)}, u32[]{:S(2)}, u32[]{:S(2)}) collective-permute-start(f32[8,1024]{1,0:T(8,128)S(1)} %get-tuple-element.26), channel_id=1, source_target_pairs={{0,16},{1,17},{2,18},{3,19},{4,20},{5,21},{6,22},{7,23},{8,24},{9,... | collective-permute-start | bytes 98312 | tf_op jit(solution)/shard_map/ppermute | solution.py:175
  9.0 0.0 collective-permute-start.2
  9.0 1.7 %collective-permute-start.9 = (f32[128,1024]{1,0:T(8,128)S(1)}, f32[128,1024]{1,0:T(8,128)S(1)}, u32[]{:S(2)}, u32[]{:S(2)}) collective-permute-start(f32[128,1024]{1,0:T(8,128)S(1)} %get-tuple-element.35), channel_id=1, source_target_pairs={{0,1},{1,0},{2,3},{3,2},{4,5},{5,4},{6,7},{7,6},{8,9},{9,8},{10,11... | collective-permute-start | bytes 1572872 | tf_op jit(solution)/shard_map/ppermute | solution.py:175
  10.7 0.2 collective-permute-done.1
  11.0 2.3 %collective-permute-start.5 = (f32[32,1024]{1,0:T(8,128)S(1)}, f32[32,1024]{1,0:T(8,128)S(1)}, u32[]{:S(2)}, u32[]{:S(2)}) collective-permute-start(f32[32,1024]{1,0:T(8,128)S(1)} %get-tuple-element.32), channel_id=1, source_target_pairs={{0,6},{1,7},{2,4},{3,5},{4,2},{5,3},{6,0},{7,1},{8,14},{9,15},{10,... | collective-permute-start | bytes 393224 | tf_op jit(solution)/shard_map/ppermute | solution.py:175
  13.2 0.0 collective-permute-done.2
  13.2 0.0 collective-permute-done
  13.2 0.0 collective-permute-done.3.z1_ref
  13.2 0.0 copy-start.1
  13.3 0.0 copy-start
  13.3 2.5 %collective-permute-start.4 = (f32[96,1024]{1,0:T(8,128)S(1)}, f32[96,1024]{1,0:T(8,128)S(1)}, u32[]{:S(2)}, u32[]{:S(2)}) collective-permute-start(f32[96,1024]{1,0:T(8,128)S(1)} %pad_maximum_fusion), channel_id=1, source_target_pairs={{0,1},{1,0},{2,3},{3,2},{4,5},{5,4},{6,7},{7,6},{8,9},{9,8},{10,11... | collective-permute-start | bytes 1179656 | tf_op jit(solution)/shard_map/ppermute | solution.py:175
  15.8 3.4 %collective-permute-start.7 = (f32[64,1024]{1,0:T(8,128)S(1)}, f32[64,1024]{1,0:T(8,128)S(1)}, u32[]{:S(2)}, u32[]{:S(2)}) collective-permute-start(f32[64,1024]{1,0:T(8,128)S(1)} %pad_maximum_fusion.1), channel_id=1, source_target_pairs={{0,4},{1,5},{2,6},{3,7},{4,0},{5,1},{6,2},{7,3},{8,12},{9,13},{10,... | collective-permute-start | bytes 786440 | tf_op jit(solution)/shard_map/ppermute | solution.py:175
  19.2 0.1 collective-permute-start.6
  19.3 0.0 collective-permute-done.9.s2_ref
  19.3 0.3 collective-permute-start.8
  19.6 0.0 copy-start.2
  19.6 3.8 %shard_map.56 = (bf16[2,512,512]{2,1,0:T(8,128)(2,1)S(1)}, f32[8,512]{1,0:T(8,128)S(1)}, f32[8,512]{1,0:T(8,128)S(1)}, f32[512,512]{1,0:T(8,128)S(1)}) custom-call(bf16[512,512]{1,0:T(8,128)(2,1)S(1)} %copy-done, bf16[512,512]{1,0:T(8,128)(2,1)S(1)} %copy-done.1, bf16[512,512]{1,0:T(8,128)(2,1)S(1)} %get-tuple-element.33.k_ref, ...), custom_call_target="tpu_custom_call" | custom-call | tf_op jit(solution)/shard_map/pallas_call | solution.py:24
  23.4 0.0 collective-permute-done.5.refs_8_
  23.4 4.6 %collective-permute-done.6.refs_2_ = f32[32,1024]{1,0:T(8,128)S(1)} collective-permute-done((f32[32,1024]{1,0:T(8,128)S(1)}, f32[32,1024]{1,0:T(8,128)S(1)}, u32[]{:S(2)}, u32[]{:S(2)}) %collective-permute-start.6) | collective-permute-done | bytes 131104 | tf_op jit(solution)/shard_map/ppermute | solution.py:175
  28.0 0.8 %collective-permute-done.8.refs_6_ = f32[32,1024]{1,0:T(8,128)S(1)} collective-permute-done((f32[32,1024]{1,0:T(8,128)S(1)}, f32[32,1024]{1,0:T(8,128)S(1)}, u32[]{:S(2)}, u32[]{:S(2)}) %collective-permute-start.8) | collective-permute-done | bytes 131104 | tf_op jit(solution)/shard_map/ppermute | solution.py:175
  28.8 0.5 %collective-permute-start.11 = (f32[64,1024]{1,0:T(8,128)S(1)}, f32[64,1024]{1,0:T(8,128)S(1)}, u32[]{:S(2)}, u32[]{:S(2)}) collective-permute-start(f32[64,1024]{1,0:T(8,128)S(1)} %collective-permute-done.7.refs_4_), channel_id=1, source_target_pairs={{0,1},{1,0},{2,3},{3,2},{4,5},{5,4},{6,7},{7,6},{8,9},{9,8},{10,11... | collective-permute-start | bytes 786440 | tf_op jit(solution)/shard_map/ppermute | solution.py:175
  29.3 0.0 collective-permute-start.10
  29.3 0.5 %collective-permute-start.12 = (f32[32,1024]{1,0:T(8,128)S(1)}, f32[32,1024]{1,0:T(8,128)S(1)}, u32[]{:S(2)}, u32[]{:S(2)}) collective-permute-start(f32[32,1024]{1,0:T(8,128)S(1)} %collective-permute-done.8.refs_6_), channel_id=1, source_target_pairs={{0,1},{1,0},{2,3},{3,2},{4,5},{5,4},{6,7},{7,6},{8,9},{9,8},{10,11... | collective-permute-start | bytes 393224 | tf_op jit(solution)/shard_map/ppermute | solution.py:175
  29.8 0.0 collective-permute-start.13
  29.8 0.8 %collective-permute-done.10.refs_3_ = f32[32,1024]{1,0:T(8,128)S(1)} collective-permute-done((f32[32,1024]{1,0:T(8,128)S(1)}, f32[32,1024]{1,0:T(8,128)S(1)}, u32[]{:S(2)}, u32[]{:S(2)}) %collective-permute-start.10) | collective-permute-done | bytes 131104 | tf_op jit(solution)/shard_map/ppermute | solution.py:175
  30.6 0.2 collective-permute-done.12.refs_7_
  30.8 0.3 collective-permute-done.13.refs_9_
  31.1 0.0 collective-permute-done.11.refs_5_
  31.1 3.2 %shard_map.57 = bf16[512,512]{1,0:T(8,128)(2,1)} custom-call(f32[32,1024]{1,0:T(8,128)S(1)} %constant_dynamic-update-slice_fusion.refs_0_, f32[96,1024]{1,0:T(8,128)S(1)} %collective-permute-done.4.near_ref.refs_1_, f32[32,1024]{1,0:T(8,128)S(1)} %collective-permute-done.6.refs_2_, f32[32,1024]{1,0:T(8,128)S(1)} %collective-permute-done.10.refs_3_, ...), custom_call_target="tpu_custom_call" | custom-call | tf_op jit(solution)/shard_map/pallas_call | solution.py:24
  (10 shorter events, 0.1 us)
Async XLA Ops:
  2.5 10.7 %collective-permute-start.3 = (f32[64,1024]{1,0:T(8,128)S(1)}, f32[64,1024]{1,0:T(8,128)S(1)}, u32[]{:S(2)}, u32[]{:S(2)}) collective-permute-start(f32[64,1024]{1,0:T(8,128)S(1)} %get-tuple-element.27), channel_id=1, source_target_pairs={{0,2},{1,3},{2,0},{3,1},{4,6},{5,7},{6,4},{7,5},{8,10},{9,11},{10,... | collective-permute-start | bytes 786440 | tf_op jit(solution)/shard_map/ppermute | solution.py:175
  5.1 8.2 %collective-permute-start = (f32[16,1024]{1,0:T(8,128)S(1)}, f32[16,1024]{1,0:T(8,128)S(1)}, u32[]{:S(2)}, u32[]{:S(2)}) collective-permute-start(f32[16,1024]{1,0:T(8,128)S(1)} %get-tuple-element.25), channel_id=1, source_target_pairs={{0,8},{1,9},{2,10},{3,11},{4,12},{5,13},{6,14},{7,15},{8,0},{9,1},... | collective-permute-start | bytes 196616 | tf_op jit(solution)/shard_map/ppermute | solution.py:175
  6.4 4.6 %collective-permute-start.1 = (f32[8,1024]{1,0:T(8,128)S(1)}, f32[8,1024]{1,0:T(8,128)S(1)}, u32[]{:S(2)}, u32[]{:S(2)}) collective-permute-start(f32[8,1024]{1,0:T(8,128)S(1)} %get-tuple-element.26), channel_id=1, source_target_pairs={{0,16},{1,17},{2,18},{3,19},{4,20},{5,21},{6,22},{7,23},{8,24},{9,... | collective-permute-start | bytes 98312 | tf_op jit(solution)/shard_map/ppermute | solution.py:175
  9.0 4.3 %collective-permute-start.2 = (f32[8,1024]{1,0:T(8,128)S(1)}, f32[8,1024]{1,0:T(8,128)S(1)}, u32[]{:S(2)}, u32[]{:S(2)}) collective-permute-start(f32[8,1024]{1,0:T(8,128)S(1)} %get-tuple-element.26), channel_id=1, source_target_pairs={{0,24},{1,25},{2,26},{3,27},{4,28},{5,29},{6,30},{7,31},{8,16},{9,... | collective-permute-start | bytes 98312 | tf_op jit(solution)/shard_map/ppermute | solution.py:175
  9.0 10.3 %collective-permute-start.9 = (f32[128,1024]{1,0:T(8,128)S(1)}, f32[128,1024]{1,0:T(8,128)S(1)}, u32[]{:S(2)}, u32[]{:S(2)}) collective-permute-start(f32[128,1024]{1,0:T(8,128)S(1)} %get-tuple-element.35), channel_id=1, source_target_pairs={{0,1},{1,0},{2,3},{3,2},{4,5},{5,4},{6,7},{7,6},{8,9},{9,8},{10,11... | collective-permute-start | bytes 1572872 | tf_op jit(solution)/shard_map/ppermute | solution.py:175
  11.0 12.5 %collective-permute-start.5 = (f32[32,1024]{1,0:T(8,128)S(1)}, f32[32,1024]{1,0:T(8,128)S(1)}, u32[]{:S(2)}, u32[]{:S(2)}) collective-permute-start(f32[32,1024]{1,0:T(8,128)S(1)} %get-tuple-element.32), channel_id=1, source_target_pairs={{0,6},{1,7},{2,4},{3,5},{4,2},{5,3},{6,0},{7,1},{8,14},{9,15},{10,... | collective-permute-start | bytes 393224 | tf_op jit(solution)/shard_map/ppermute | solution.py:175
  13.2 6.3 %copy-start.1 = (bf16[512,512]{1,0:T(8,128)(2,1)S(1)}, bf16[512,512]{1,0:T(8,128)(2,1)}, u32[]{:S(2)}) copy-start(bf16[512,512]{1,0:T(8,128)(2,1)} %wq_ref.1) | copy-start | bytes 1572868
  13.3 6.3 %copy-start = (bf16[512,512]{1,0:T(8,128)(2,1)S(1)}, bf16[512,512]{1,0:T(8,128)(2,1)}, u32[]{:S(2)}) copy-start(bf16[512,512]{1,0:T(8,128)(2,1)} %x_ref.1) | copy-start | bytes 1572868
  13.3 6.3 %collective-permute-start.4 = (f32[96,1024]{1,0:T(8,128)S(1)}, f32[96,1024]{1,0:T(8,128)S(1)}, u32[]{:S(2)}, u32[]{:S(2)}) collective-permute-start(f32[96,1024]{1,0:T(8,128)S(1)} %pad_maximum_fusion), channel_id=1, source_target_pairs={{0,1},{1,0},{2,3},{3,2},{4,5},{5,4},{6,7},{7,6},{8,9},{9,8},{10,11... | collective-permute-start | bytes 1179656 | tf_op jit(solution)/shard_map/ppermute | solution.py:175
  15.8 13.0 %collective-permute-start.7 = (f32[64,1024]{1,0:T(8,128)S(1)}, f32[64,1024]{1,0:T(8,128)S(1)}, u32[]{:S(2)}, u32[]{:S(2)}) collective-permute-start(f32[64,1024]{1,0:T(8,128)S(1)} %pad_maximum_fusion.1), channel_id=1, source_target_pairs={{0,4},{1,5},{2,6},{3,7},{4,0},{5,1},{6,2},{7,3},{8,12},{9,13},{10,... | collective-permute-start | bytes 786440 | tf_op jit(solution)/shard_map/ppermute | solution.py:175
  19.2 8.8 %collective-permute-start.6 = (f32[32,1024]{1,0:T(8,128)S(1)}, f32[32,1024]{1,0:T(8,128)S(1)}, u32[]{:S(2)}, u32[]{:S(2)}) collective-permute-start(f32[32,1024]{1,0:T(8,128)S(1)} %constant_dynamic-update-slice_fusion.refs_0_), channel_id=1, source_target_pairs={{0,2},{1,3},{2,0},{3,1},{4,6},{5,7},{6,4},{7,5},{8,10},{9,11},{10,... | collective-permute-start | bytes 393224 | tf_op jit(solution)/shard_map/ppermute | solution.py:175
  19.3 9.5 %collective-permute-start.8 = (f32[32,1024]{1,0:T(8,128)S(1)}, f32[32,1024]{1,0:T(8,128)S(1)}, u32[]{:S(2)}, u32[]{:S(2)}) collective-permute-start(f32[32,1024]{1,0:T(8,128)S(1)} %constant_dynamic-update-slice_fusion.refs_0_), channel_id=1, source_target_pairs={{0,6},{1,7},{2,4},{3,5},{4,2},{5,3},{6,0},{7,1},{8,14},{9,15},{10,... | collective-permute-start | bytes 393224 | tf_op jit(solution)/shard_map/ppermute | solution.py:175
  19.6 11.5 %copy-start.2 = (bf16[512,512]{1,0:T(8,128)(2,1)S(1)}, bf16[512,512]{1,0:T(8,128)(2,1)}, u32[]{:S(2)}) copy-start(bf16[512,512]{1,0:T(8,128)(2,1)} %refs_14_.1) | copy-start | bytes 1572868
  28.8 2.3 %collective-permute-start.11 = (f32[64,1024]{1,0:T(8,128)S(1)}, f32[64,1024]{1,0:T(8,128)S(1)}, u32[]{:S(2)}, u32[]{:S(2)}) collective-permute-start(f32[64,1024]{1,0:T(8,128)S(1)} %collective-permute-done.7.refs_4_), channel_id=1, source_target_pairs={{0,1},{1,0},{2,3},{3,2},{4,5},{5,4},{6,7},{7,6},{8,9},{9,8},{10,11... | collective-permute-start | bytes 786440 | tf_op jit(solution)/shard_map/ppermute | solution.py:175
  29.3 1.3 %collective-permute-start.10 = (f32[32,1024]{1,0:T(8,128)S(1)}, f32[32,1024]{1,0:T(8,128)S(1)}, u32[]{:S(2)}, u32[]{:S(2)}) collective-permute-start(f32[32,1024]{1,0:T(8,128)S(1)} %collective-permute-done.6.refs_2_), channel_id=1, source_target_pairs={{0,1},{1,0},{2,3},{3,2},{4,5},{5,4},{6,7},{7,6},{8,9},{9,8},{10,11... | collective-permute-start | bytes 393224 | tf_op jit(solution)/shard_map/ppermute | solution.py:175
  29.3 1.5 %collective-permute-start.12 = (f32[32,1024]{1,0:T(8,128)S(1)}, f32[32,1024]{1,0:T(8,128)S(1)}, u32[]{:S(2)}, u32[]{:S(2)}) collective-permute-start(f32[32,1024]{1,0:T(8,128)S(1)} %collective-permute-done.8.refs_6_), channel_id=1, source_target_pairs={{0,1},{1,0},{2,3},{3,2},{4,5},{5,4},{6,7},{7,6},{8,9},{9,8},{10,11... | collective-permute-start | bytes 393224 | tf_op jit(solution)/shard_map/ppermute | solution.py:175
  29.8 1.3 %collective-permute-start.13 = (f32[32,1024]{1,0:T(8,128)S(1)}, f32[32,1024]{1,0:T(8,128)S(1)}, u32[]{:S(2)}, u32[]{:S(2)}) collective-permute-start(f32[32,1024]{1,0:T(8,128)S(1)} %collective-permute-done.5.refs_8_), channel_id=1, source_target_pairs={{0,1},{1,0},{2,3},{3,2},{4,5},{5,4},{6,7},{7,6},{8,9},{9,8},{10,11... | collective-permute-start | bytes 393224 | tf_op jit(solution)/shard_map/ppermute | solution.py:175

commit v4 on v3

--- a/solution.py
+++ b/solution.py
@@ -174,6 +174,9 @@
     def swap(block, apart):
         return lax.ppermute(block, "seq", [(i, i ^ apart) for i in range(count)])
 
+    def beyond(block):
+        return lax.ppermute(block, "seq", [(i, i ^ (24 if i & 1 else 16)) for i in range(count)])
+
     k, v, c2, c3, c4, c5, c6 = call(
         project_kernel,
         [shape(rows, D, dtype=BF16)] * 2 + [shape(rows >> l, 2 * D) for l in range(2, 7)],
@@ -184,9 +187,10 @@
         place=HBM,
     )
     z1, z3 = swap(c3, 2), swap(c4, 6)
-    y1, y2, y3 = swap(c5, 8), swap(c6, 16), swap(c6, 24)
-    y1, y2, y3, z1 = lax.optimization_barrier((y1, y2, y3, z1))
-    g = jnp.concatenate([y1, y2, y3], axis=0)
+    y1 = swap(c5, 8)
+    y2 = beyond(jnp.concatenate([c6, swap(c6, 1)], axis=0))
+    y1, y2, z1 = lax.optimization_barrier((y1, y2, z1))
+    g = jnp.concatenate([y1, y2], axis=0)
     near = swap(jnp.concatenate([z1, g], axis=0), 1)
     s2 = swap(c2, 1)
     g2 = swap(jnp.concatenate([g, c4], axis=0), 4)

time: 34.4 us -> 32.4 us (0.942)
  starting transfers between devices: 17.7 us -> 16 us
    ppermute x14 -> x13, starting transfers between devices: 17.7 us -> 13.7 us  [swap(): return lax.ppermute(block, 'seq', [(i, i ^ apart) for i in range(count)])]
    ppermute x0 -> x1, starting transfers between devices: none -> 2.28 us  [beyond(): lax.ppermute(block, 'seq', [(i, i ^ (24 if i & 1 else 16)) for i in range...]
    ppermute x14 -> x13, waiting for transfers between devices: 6.91 us -> 6.66 us  [swap(): return lax.ppermute(block, 'seq', [(i, i ^ apart) for i in range(count)])]
  transfers between devices with their start and end apart: 14 -> 14, of which waited for: 6 -> 5; matrix products, arithmetic and copies ran while one was open for 0% -> 0% of each run, Pallas kernels for 11% -> 12%
where the time goes in v4:
time: 32.4 us; the launch traced here: 32.3 us
  starting transfers between devices  16 us (49%)
  Pallas kernels  9.5 us (29%)
  waiting for transfers between devices  6.66 us (21%)
    ppermute x13, starting transfers between devices, swap(): return lax.ppermute(block, 'seq', [(i, i ^ apart) for i in range(count)])  13.7 us
    pallas_call x3, Pallas kernels, call(): pl.pallas_call(body, out_shape=outs, in_specs=[place] * len(args), out_sp...  9.5 us
    ppermute x13, waiting for transfers between devices, swap(): return lax.ppermute(block, 'seq', [(i, i ^ apart) for i in range(count)])  6.66 us
    ppermute x1, starting transfers between devices, beyond(): lax.ppermute(block, 'seq', [(i, i ^ (24 if i & 1 else 16)) for i in range...  2.28 us
  transfers between devices with their start and end apart: 14, of which 5 were waited for; matrix products, arithmetic and copies ran while one was open for 0% of the time, Pallas kernels for 12%

profile of v4, /device:TPU:1, one launch (start us, length us, event | category | flops | bytes accessed | tf_op | source)
XLA Modules:
  0.0 32.3 jit_solution(7769878448871759422)
XLA Ops:
  0.0 2.5 %shard_map.55 = (bf16[512,512]{1,0:T(8,128)(2,1)S(1)}, bf16[512,512]{1,0:T(8,128)(2,1)S(1)}, f32[128,1024]{1,0:T(8,128)S(1)}, f32[64,1024]{1,0:T(8,128)S(1)}, f3...) custom-call(bf16[512,512]{1,0:T(8,128)(2,1)} %x_ref.1, bf16[512,512]{1,0:T(8,128)(2,1)} %wk_hbm.1, ...), custom_call_target="tpu_custom_call" | custom-call | tf_op jit(solution)/shard_map/pallas_call | solution.py:24
  2.5 2.5 %collective-permute-start.3 = (f32[64,1024]{1,0:T(8,128)S(1)}, f32[64,1024]{1,0:T(8,128)S(1)}, u32[]{:S(2)}, u32[]{:S(2)}) collective-permute-start(f32[64,1024]{1,0:T(8,128)S(1)} %get-tuple-element.26), channel_id=1, source_target_pairs={{0,2},{1,3},{2,0},{3,1},{4,6},{5,7},{6,4},{7,5},{8,10},{9,11},{10,... | collective-permute-start | bytes 786440 | tf_op jit(solution)/shard_map/ppermute | solution.py:175
  5.1 1.0 %collective-permute-start.1 = (f32[8,1024]{1,0:T(8,128)S(1)}, f32[8,1024]{1,0:T(8,128)S(1)}, u32[]{:S(2)}, u32[]{:S(2)}) collective-permute-start(f32[8,1024]{1,0:T(8,128)S(1)} %get-tuple-element.25), channel_id=1, source_target_pairs={{0,1},{1,0},{2,3},{3,2},{4,5},{5,4},{6,7},{7,6},{8,9},{9,8},{10,11... | collective-permute-start | bytes 98312 | tf_op jit(solution)/shard_map/ppermute | solution.py:175
  6.0 1.3 %collective-permute-start = (f32[16,1024]{1,0:T(8,128)S(1)}, f32[16,1024]{1,0:T(8,128)S(1)}, u32[]{:S(2)}, u32[]{:S(2)}) collective-permute-start(f32[16,1024]{1,0:T(8,128)S(1)} %get-tuple-element.24), channel_id=1, source_target_pairs={{0,8},{1,9},{2,10},{3,11},{4,12},{5,13},{6,14},{7,15},{8,0},{9,1},... | collective-permute-start | bytes 196616 | tf_op jit(solution)/shard_map/ppermute | solution.py:175
  7.3 0.0 collective-permute-done.1
  7.3 2.3 %collective-permute-start.2 = (f32[16,1024]{1,0:T(8,128)S(1)}, f32[16,1024]{1,0:T(8,128)S(1)}, u32[]{:S(2)}, u32[]{:S(2)}) collective-permute-start(f32[16,1024]{1,0:T(8,128)S(1)} %pad_maximum_fusion.2), channel_id=1, source_target_pairs={{0,16},{1,25},{2,18},{3,27},{4,20},{5,29},{6,22},{7,31},{8,24},{9,... | collective-permute-start | bytes 196616 | tf_op jit(solution)/shard_map/ppermute | solution.py:178
  9.6 1.0 %collective-permute-start.9 = (f32[128,1024]{1,0:T(8,128)S(1)}, f32[128,1024]{1,0:T(8,128)S(1)}, u32[]{:S(2)}, u32[]{:S(2)}) collective-permute-start(f32[128,1024]{1,0:T(8,128)S(1)} %get-tuple-element.33), channel_id=1, source_target_pairs={{0,1},{1,0},{2,3},{3,2},{4,5},{5,4},{6,7},{7,6},{8,9},{9,8},{10,11... | collective-permute-start | bytes 1572872 | tf_op jit(solution)/shard_map/ppermute | solution.py:175
  10.6 2.2 %collective-permute-start.5 = (f32[32,1024]{1,0:T(8,128)S(1)}, f32[32,1024]{1,0:T(8,128)S(1)}, u32[]{:S(2)}, u32[]{:S(2)}) collective-permute-start(f32[32,1024]{1,0:T(8,128)S(1)} %get-tuple-element.30), channel_id=1, source_target_pairs={{0,6},{1,7},{2,4},{3,5},{4,2},{5,3},{6,0},{7,1},{8,14},{9,15},{10,... | collective-permute-start | bytes 393224 | tf_op jit(solution)/shard_map/ppermute | solution.py:175
  12.8 0.0 collective-permute-done.2
  12.9 0.0 collective-permute-done.3.z1_ref
  12.9 0.0 copy-start.1
  12.9 0.0 copy-start
  12.9 0.9 %collective-permute-start.4 = (f32[96,1024]{1,0:T(8,128)S(1)}, f32[96,1024]{1,0:T(8,128)S(1)}, u32[]{:S(2)}, u32[]{:S(2)}) collective-permute-start(f32[96,1024]{1,0:T(8,128)S(1)} %pad_maximum_fusion), channel_id=1, source_target_pairs={{0,1},{1,0},{2,3},{3,2},{4,5},{5,4},{6,7},{7,6},{8,9},{9,8},{10,11... | collective-permute-start | bytes 1179656 | tf_op jit(solution)/shard_map/ppermute | solution.py:175
  13.8 3.4 %collective-permute-start.7 = (f32[64,1024]{1,0:T(8,128)S(1)}, f32[64,1024]{1,0:T(8,128)S(1)}, u32[]{:S(2)}, u32[]{:S(2)}) collective-permute-start(f32[64,1024]{1,0:T(8,128)S(1)} %pad_maximum_fusion.1), channel_id=1, source_target_pairs={{0,4},{1,5},{2,6},{3,7},{4,0},{5,1},{6,2},{7,3},{8,12},{9,13},{10,... | collective-permute-start | bytes 786440 | tf_op jit(solution)/shard_map/ppermute | solution.py:175
  17.2 0.1 collective-permute-start.6
  17.3 0.0 collective-permute-done.9.s2_ref
  17.3 0.3 collective-permute-start.8
  17.6 0.0 collective-permute-done.4.near_ref.refs_1_
  17.6 0.0 copy-start.2
  17.6 3.8 %shard_map.56 = (bf16[2,512,512]{2,1,0:T(8,128)(2,1)S(1)}, f32[8,512]{1,0:T(8,128)S(1)}, f32[8,512]{1,0:T(8,128)S(1)}, f32[512,512]{1,0:T(8,128)S(1)}) custom-call(bf16[512,512]{1,0:T(8,128)(2,1)S(1)} %copy-done, bf16[512,512]{1,0:T(8,128)(2,1)S(1)} %copy-done.1, bf16[512,512]{1,0:T(8,128)(2,1)S(1)} %get-tuple-element.31.k_ref, ...), custom_call_target="tpu_custom_call" | custom-call | tf_op jit(solution)/shard_map/pallas_call | solution.py:24
  21.5 0.0 collective-permute-done.5.refs_8_
  21.5 4.6 %collective-permute-done.6.refs_2_ = f32[32,1024]{1,0:T(8,128)S(1)} collective-permute-done((f32[32,1024]{1,0:T(8,128)S(1)}, f32[32,1024]{1,0:T(8,128)S(1)}, u32[]{:S(2)}, u32[]{:S(2)}) %collective-permute-start.6) | collective-permute-done | bytes 131104 | tf_op jit(solution)/shard_map/ppermute | solution.py:175
  26.0 0.8 %collective-permute-done.8.refs_6_ = f32[32,1024]{1,0:T(8,128)S(1)} collective-permute-done((f32[32,1024]{1,0:T(8,128)S(1)}, f32[32,1024]{1,0:T(8,128)S(1)}, u32[]{:S(2)}, u32[]{:S(2)}) %collective-permute-start.8) | collective-permute-done | bytes 131104 | tf_op jit(solution)/shard_map/ppermute | solution.py:175
  26.8 0.0 collective-permute-done.7.refs_4_
  26.8 0.5 %collective-permute-start.11 = (f32[64,1024]{1,0:T(8,128)S(1)}, f32[64,1024]{1,0:T(8,128)S(1)}, u32[]{:S(2)}, u32[]{:S(2)}) collective-permute-start(f32[64,1024]{1,0:T(8,128)S(1)} %collective-permute-done.7.refs_4_), channel_id=1, source_target_pairs={{0,1},{1,0},{2,3},{3,2},{4,5},{5,4},{6,7},{7,6},{8,9},{9,8},{10,11... | collective-permute-start | bytes 786440 | tf_op jit(solution)/shard_map/ppermute | solution.py:175
  27.3 0.0 collective-permute-start.10
  27.3 0.5 %collective-permute-start.12 = (f32[32,1024]{1,0:T(8,128)S(1)}, f32[32,1024]{1,0:T(8,128)S(1)}, u32[]{:S(2)}, u32[]{:S(2)}) collective-permute-start(f32[32,1024]{1,0:T(8,128)S(1)} %collective-permute-done.8.refs_6_), channel_id=1, source_target_pairs={{0,1},{1,0},{2,3},{3,2},{4,5},{5,4},{6,7},{7,6},{8,9},{9,8},{10,11... | collective-permute-start | bytes 393224 | tf_op jit(solution)/shard_map/ppermute | solution.py:175
  27.8 0.0 collective-permute-start.13
  27.8 0.8 %collective-permute-done.10.refs_3_ = f32[32,1024]{1,0:T(8,128)S(1)} collective-permute-done((f32[32,1024]{1,0:T(8,128)S(1)}, f32[32,1024]{1,0:T(8,128)S(1)}, u32[]{:S(2)}, u32[]{:S(2)}) %collective-permute-start.10) | collective-permute-done | bytes 131104 | tf_op jit(solution)/shard_map/ppermute | solution.py:175
  28.6 0.2 collective-permute-done.12.refs_7_
  28.8 0.3 collective-permute-done.13.refs_9_
  29.2 3.2 %shard_map.57 = bf16[512,512]{1,0:T(8,128)(2,1)} custom-call(f32[32,1024]{1,0:T(8,128)S(1)} %constant_dynamic-update-slice_fusion.refs_0_, f32[96,1024]{1,0:T(8,128)S(1)} %collective-permute-done.4.near_ref.refs_1_, f32[32,1024]{1,0:T(8,128)S(1)} %collective-permute-done.6.refs_2_, f32[32,1024]{1,0:T(8,128)S(1)} %collective-permute-done.10.refs_3_, ...), custom_call_target="tpu_custom_call" | custom-call | tf_op jit(solution)/shard_map/pallas_call | solution.py:24
  (10 shorter events, 0.1 us)
Async XLA Ops:
  2.5 10.3 %collective-permute-start.3 = (f32[64,1024]{1,0:T(8,128)S(1)}, f32[64,1024]{1,0:T(8,128)S(1)}, u32[]{:S(2)}, u32[]{:S(2)}) collective-permute-start(f32[64,1024]{1,0:T(8,128)S(1)} %get-tuple-element.26), channel_id=1, source_target_pairs={{0,2},{1,3},{2,0},{3,1},{4,6},{5,7},{6,4},{7,5},{8,10},{9,11},{10,... | collective-permute-start | bytes 786440 | tf_op jit(solution)/shard_map/ppermute | solution.py:175
  5.1 2.3 %collective-permute-start.1 = (f32[8,1024]{1,0:T(8,128)S(1)}, f32[8,1024]{1,0:T(8,128)S(1)}, u32[]{:S(2)}, u32[]{:S(2)}) collective-permute-start(f32[8,1024]{1,0:T(8,128)S(1)} %get-tuple-element.25), channel_id=1, source_target_pairs={{0,1},{1,0},{2,3},{3,2},{4,5},{5,4},{6,7},{7,6},{8,9},{9,8},{10,11... | collective-permute-start | bytes 98312 | tf_op jit(solution)/shard_map/ppermute | solution.py:175
  6.0 6.8 %collective-permute-start = (f32[16,1024]{1,0:T(8,128)S(1)}, f32[16,1024]{1,0:T(8,128)S(1)}, u32[]{:S(2)}, u32[]{:S(2)}) collective-permute-start(f32[16,1024]{1,0:T(8,128)S(1)} %get-tuple-element.24), channel_id=1, source_target_pairs={{0,8},{1,9},{2,10},{3,11},{4,12},{5,13},{6,14},{7,15},{8,0},{9,1},... | collective-permute-start | bytes 196616 | tf_op jit(solution)/shard_map/ppermute | solution.py:175
  7.3 5.5 %collective-permute-start.2 = (f32[16,1024]{1,0:T(8,128)S(1)}, f32[16,1024]{1,0:T(8,128)S(1)}, u32[]{:S(2)}, u32[]{:S(2)}) collective-permute-start(f32[16,1024]{1,0:T(8,128)S(1)} %pad_maximum_fusion.2), channel_id=1, source_target_pairs={{0,16},{1,25},{2,18},{3,27},{4,20},{5,29},{6,22},{7,31},{8,24},{9,... | collective-permute-start | bytes 196616 | tf_op jit(solution)/shard_map/ppermute | solution.py:178
  9.6 7.7 %collective-permute-start.9 = (f32[128,1024]{1,0:T(8,128)S(1)}, f32[128,1024]{1,0:T(8,128)S(1)}, u32[]{:S(2)}, u32[]{:S(2)}) collective-permute-start(f32[128,1024]{1,0:T(8,128)S(1)} %get-tuple-element.33), channel_id=1, source_target_pairs={{0,1},{1,0},{2,3},{3,2},{4,5},{5,4},{6,7},{7,6},{8,9},{9,8},{10,11... | collective-permute-start | bytes 1572872 | tf_op jit(solution)/shard_map/ppermute | solution.py:175
  10.6 10.9 %collective-permute-start.5 = (f32[32,1024]{1,0:T(8,128)S(1)}, f32[32,1024]{1,0:T(8,128)S(1)}, u32[]{:S(2)}, u32[]{:S(2)}) collective-permute-start(f32[32,1024]{1,0:T(8,128)S(1)} %get-tuple-element.30), channel_id=1, source_target_pairs={{0,6},{1,7},{2,4},{3,5},{4,2},{5,3},{6,0},{7,1},{8,14},{9,15},{10,... | collective-permute-start | bytes 393224 | tf_op jit(solution)/shard_map/ppermute | solution.py:175
  12.9 4.8 %copy-start.1 = (bf16[512,512]{1,0:T(8,128)(2,1)S(1)}, bf16[512,512]{1,0:T(8,128)(2,1)}, u32[]{:S(2)}) copy-start(bf16[512,512]{1,0:T(8,128)(2,1)} %wq_ref.1) | copy-start | bytes 1572868
  12.9 4.7 %copy-start = (bf16[512,512]{1,0:T(8,128)(2,1)S(1)}, bf16[512,512]{1,0:T(8,128)(2,1)}, u32[]{:S(2)}) copy-start(bf16[512,512]{1,0:T(8,128)(2,1)} %x_ref.1) | copy-start | bytes 1572868
  12.9 4.7 %collective-permute-start.4 = (f32[96,1024]{1,0:T(8,128)S(1)}, f32[96,1024]{1,0:T(8,128)S(1)}, u32[]{:S(2)}, u32[]{:S(2)}) collective-permute-start(f32[96,1024]{1,0:T(8,128)S(1)} %pad_maximum_fusion), channel_id=1, source_target_pairs={{0,1},{1,0},{2,3},{3,2},{4,5},{5,4},{6,7},{7,6},{8,9},{9,8},{10,11... | collective-permute-start | bytes 1179656 | tf_op jit(solution)/shard_map/ppermute | solution.py:175
  13.8 13.0 %collective-permute-start.7 = (f32[64,1024]{1,0:T(8,128)S(1)}, f32[64,1024]{1,0:T(8,128)S(1)}, u32[]{:S(2)}, u32[]{:S(2)}) collective-permute-start(f32[64,1024]{1,0:T(8,128)S(1)} %pad_maximum_fusion.1), channel_id=1, source_target_pairs={{0,4},{1,5},{2,6},{3,7},{4,0},{5,1},{6,2},{7,3},{8,12},{9,13},{10,... | collective-permute-start | bytes 786440 | tf_op jit(solution)/shard_map/ppermute | solution.py:175
  17.2 8.8 %collective-permute-start.6 = (f32[32,1024]{1,0:T(8,128)S(1)}, f32[32,1024]{1,0:T(8,128)S(1)}, u32[]{:S(2)}, u32[]{:S(2)}) collective-permute-start(f32[32,1024]{1,0:T(8,128)S(1)} %constant_dynamic-update-slice_fusion.refs_0_), channel_id=1, source_target_pairs={{0,2},{1,3},{2,0},{3,1},{4,6},{5,7},{6,4},{7,5},{8,10},{9,11},{10,... | collective-permute-start | bytes 393224 | tf_op jit(solution)/shard_map/ppermute | solution.py:175
  17.3 9.5 %collective-permute-start.8 = (f32[32,1024]{1,0:T(8,128)S(1)}, f32[32,1024]{1,0:T(8,128)S(1)}, u32[]{:S(2)}, u32[]{:S(2)}) collective-permute-start(f32[32,1024]{1,0:T(8,128)S(1)} %constant_dynamic-update-slice_fusion.refs_0_), channel_id=1, source_target_pairs={{0,6},{1,7},{2,4},{3,5},{4,2},{5,3},{6,0},{7,1},{8,14},{9,15},{10,... | collective-permute-start | bytes 393224 | tf_op jit(solution)/shard_map/ppermute | solution.py:175
  17.6 11.5 %copy-start.2 = (bf16[512,512]{1,0:T(8,128)(2,1)S(1)}, bf16[512,512]{1,0:T(8,128)(2,1)}, u32[]{:S(2)}) copy-start(bf16[512,512]{1,0:T(8,128)(2,1)} %refs_14_.1) | copy-start | bytes 1572868
  26.8 2.3 %collective-permute-start.11 = (f32[64,1024]{1,0:T(8,128)S(1)}, f32[64,1024]{1,0:T(8,128)S(1)}, u32[]{:S(2)}, u32[]{:S(2)}) collective-permute-start(f32[64,1024]{1,0:T(8,128)S(1)} %collective-permute-done.7.refs_4_), channel_id=1, source_target_pairs={{0,1},{1,0},{2,3},{3,2},{4,5},{5,4},{6,7},{7,6},{8,9},{9,8},{10,11... | collective-permute-start | bytes 786440 | tf_op jit(solution)/shard_map/ppermute | solution.py:175
  27.3 1.3 %collective-permute-start.10 = (f32[32,1024]{1,0:T(8,128)S(1)}, f32[32,1024]{1,0:T(8,128)S(1)}, u32[]{:S(2)}, u32[]{:S(2)}) collective-permute-start(f32[32,1024]{1,0:T(8,128)S(1)} %collective-permute-done.6.refs_2_), channel_id=1, source_target_pairs={{0,1},{1,0},{2,3},{3,2},{4,5},{5,4},{6,7},{7,6},{8,9},{9,8},{10,11... | collective-permute-start | bytes 393224 | tf_op jit(solution)/shard_map/ppermute | solution.py:175
  27.3 1.5 %collective-permute-start.12 = (f32[32,1024]{1,0:T(8,128)S(1)}, f32[32,1024]{1,0:T(8,128)S(1)}, u32[]{:S(2)}, u32[]{:S(2)}) collective-permute-start(f32[32,1024]{1,0:T(8,128)S(1)} %collective-permute-done.8.refs_6_), channel_id=1, source_target_pairs={{0,1},{1,0},{2,3},{3,2},{4,5},{5,4},{6,7},{7,6},{8,9},{9,8},{10,11... | collective-permute-start | bytes 393224 | tf_op jit(solution)/shard_map/ppermute | solution.py:175
  27.8 1.3 %collective-permute-start.13 = (f32[32,1024]{1,0:T(8,128)S(1)}, f32[32,1024]{1,0:T(8,128)S(1)}, u32[]{:S(2)}, u32[]{:S(2)}) collective-permute-start(f32[32,1024]{1,0:T(8,128)S(1)} %collective-permute-done.5.refs_8_), channel_id=1, source_target_pairs={{0,1},{1,0},{2,3},{3,2},{4,5},{5,4},{6,7},{7,6},{8,9},{9,8},{10,11... | collective-permute-start | bytes 393224 | tf_op jit(solution)/shard_map/ppermute | solution.py:175

commit v5 on v4

--- a/solution.py
+++ b/solution.py
@@ -215,16 +215,14 @@
         ],
     )
     z3, g1, g2, g3, top = lax.optimization_barrier((z3, g1, g2, g3, top))
-    zf = swap(z3, 1)
     def staged(slots):
         return [pltpu.VMEM((slots, BLK, D), BF16), pltpu.VMEM((slots, D, BLK), BF16)]
 
-    f1, f2, f3 = swap(g1, 1), swap(g2, 1), swap(g3, 1)
-    arrays = [g, near, g1, f1, g2, f2, g3, f3, z3, zf]
-    plan = [
-        [(i, at + (64 if i == 1 else 0), 16) for i in range(8)] for at in (0, 16)
-    ]
-    plan = [[(4, 32, 32), (5, 32, 32), (8, 0, 32), (9, 0, 32)]] + plan
+    f1, f2 = swap(jnp.concatenate([g1, g3, z3], axis=0), 1), swap(g2, 1)
+    arrays = [g, near, g1, f1, g2, f2, g3, z3]
+    parts = [(0, 0), (1, 64), (2, 0), (3, 0), (4, 0), (5, 0), (6, 0), (3, 32)]
+    plan = [[(i, lo + at, 16) for i, lo in parts] for at in (0, 16)]
+    plan = [[(4, 32, 32), (5, 32, 32), (7, 0, 32), (3, 64, 32)]] + plan
     return call(
         functools.partial(final_kernel, plan, (4, 5, 6), len(arrays)),
         shape(rows, D, dtype=BF16),

time: 32.4 us -> 32.4 us (level)
  starting transfers between devices: 16 us -> 15.6 us
    ppermute x13 -> x11, starting transfers between devices: 13.7 us -> 13.3 us  [swap(): return lax.ppermute(block, 'seq', [(i, i ^ apart) for i in range(count)])]
    ppermute x13 -> x11, waiting for transfers between devices: 6.66 us -> 6.98 us  [swap(): return lax.ppermute(block, 'seq', [(i, i ^ apart) for i in range(count)])]
  transfers between devices with their start and end apart: 14 -> 12, of which waited for: 5 -> 3; matrix products, arithmetic and copies ran while one was open for 0% -> 0% of each run, Pallas kernels for 12% -> 12%
where the time goes in v5:
time: 32.4 us; the launch traced here: 32.3 us
  starting transfers between devices  15.6 us (48%)
  Pallas kernels  9.5 us (29%)
  waiting for transfers between devices  6.98 us (22%)
    ppermute x11, starting transfers between devices, swap(): return lax.ppermute(block, 'seq', [(i, i ^ apart) for i in range(count)])  13.3 us
    pallas_call x3, Pallas kernels, call(): pl.pallas_call(body, out_shape=outs, in_specs=[place] * len(args), out_sp...  9.5 us
    ppermute x11, waiting for transfers between devices, swap(): return lax.ppermute(block, 'seq', [(i, i ^ apart) for i in range(count)])  6.98 us
    ppermute x1, starting transfers between devices, beyond(): lax.ppermute(block, 'seq', [(i, i ^ (24 if i & 1 else 16)) for i in range...  2.28 us
  transfers between devices with their start and end apart: 12, of which 3 were waited for; matrix products, arithmetic and copies ran while one was open for 0% of the time, Pallas kernels for 12%

profile of v5, /device:TPU:1, one launch (start us, length us, event | category | flops | bytes accessed | tf_op | source)
XLA Modules:
  0.0 32.3 jit_solution(6549970336186897579)
XLA Ops:
  0.0 2.5 %shard_map.55 = (bf16[512,512]{1,0:T(8,128)(2,1)S(1)}, bf16[512,512]{1,0:T(8,128)(2,1)S(1)}, f32[128,1024]{1,0:T(8,128)S(1)}, f32[64,1024]{1,0:T(8,128)S(1)}, f3...) custom-call(bf16[512,512]{1,0:T(8,128)(2,1)} %x_ref.1, bf16[512,512]{1,0:T(8,128)(2,1)} %wk_hbm.1, ...), custom_call_target="tpu_custom_call" | custom-call | tf_op jit(solution)/shard_map/pallas_call | solution.py:24
  2.5 2.5 %collective-permute-start.3 = (f32[64,1024]{1,0:T(8,128)S(1)}, f32[64,1024]{1,0:T(8,128)S(1)}, u32[]{:S(2)}, u32[]{:S(2)}) collective-permute-start(f32[64,1024]{1,0:T(8,128)S(1)} %get-tuple-element.26), channel_id=1, source_target_pairs={{0,2},{1,3},{2,0},{3,1},{4,6},{5,7},{6,4},{7,5},{8,10},{9,11},{10,... | collective-permute-start | bytes 786440 | tf_op jit(solution)/shard_map/ppermute | solution.py:175
  5.1 1.0 %collective-permute-start.1 = (f32[8,1024]{1,0:T(8,128)S(1)}, f32[8,1024]{1,0:T(8,128)S(1)}, u32[]{:S(2)}, u32[]{:S(2)}) collective-permute-start(f32[8,1024]{1,0:T(8,128)S(1)} %get-tuple-element.25), channel_id=1, source_target_pairs={{0,1},{1,0},{2,3},{3,2},{4,5},{5,4},{6,7},{7,6},{8,9},{9,8},{10,11... | collective-permute-start | bytes 98312 | tf_op jit(solution)/shard_map/ppermute | solution.py:175
  6.0 1.3 %collective-permute-start = (f32[16,1024]{1,0:T(8,128)S(1)}, f32[16,1024]{1,0:T(8,128)S(1)}, u32[]{:S(2)}, u32[]{:S(2)}) collective-permute-start(f32[16,1024]{1,0:T(8,128)S(1)} %get-tuple-element.24), channel_id=1, source_target_pairs={{0,8},{1,9},{2,10},{3,11},{4,12},{5,13},{6,14},{7,15},{8,0},{9,1},... | collective-permute-start | bytes 196616 | tf_op jit(solution)/shard_map/ppermute | solution.py:175
  7.3 0.0 collective-permute-done.1
  7.3 2.3 %collective-permute-start.2 = (f32[16,1024]{1,0:T(8,128)S(1)}, f32[16,1024]{1,0:T(8,128)S(1)}, u32[]{:S(2)}, u32[]{:S(2)}) collective-permute-start(f32[16,1024]{1,0:T(8,128)S(1)} %pad_maximum_fusion.3), channel_id=1, source_target_pairs={{0,16},{1,25},{2,18},{3,27},{4,20},{5,29},{6,22},{7,31},{8,24},{9,... | collective-permute-start | bytes 196616 | tf_op jit(solution)/shard_map/ppermute | solution.py:178
  9.6 1.0 %collective-permute-start.9 = (f32[128,1024]{1,0:T(8,128)S(1)}, f32[128,1024]{1,0:T(8,128)S(1)}, u32[]{:S(2)}, u32[]{:S(2)}) collective-permute-start(f32[128,1024]{1,0:T(8,128)S(1)} %get-tuple-element.33), channel_id=1, source_target_pairs={{0,1},{1,0},{2,3},{3,2},{4,5},{5,4},{6,7},{7,6},{8,9},{9,8},{10,11... | collective-permute-start | bytes 1572872 | tf_op jit(solution)/shard_map/ppermute | solution.py:175
  10.6 2.2 %collective-permute-start.5 = (f32[32,1024]{1,0:T(8,128)S(1)}, f32[32,1024]{1,0:T(8,128)S(1)}, u32[]{:S(2)}, u32[]{:S(2)}) collective-permute-start(f32[32,1024]{1,0:T(8,128)S(1)} %get-tuple-element.30), channel_id=1, source_target_pairs={{0,6},{1,7},{2,4},{3,5},{4,2},{5,3},{6,0},{7,1},{8,14},{9,15},{10,... | collective-permute-start | bytes 393224 | tf_op jit(solution)/shard_map/ppermute | solution.py:175
  12.8 0.0 collective-permute-done
  12.8 0.0 collective-permute-done.2
  12.9 0.0 collective-permute-done.3.z1_ref
  12.9 0.0 copy-start.1
  12.9 0.0 copy-start
  12.9 0.9 %collective-permute-start.4 = (f32[96,1024]{1,0:T(8,128)S(1)}, f32[96,1024]{1,0:T(8,128)S(1)}, u32[]{:S(2)}, u32[]{:S(2)}) collective-permute-start(f32[96,1024]{1,0:T(8,128)S(1)} %pad_maximum_fusion), channel_id=1, source_target_pairs={{0,1},{1,0},{2,3},{3,2},{4,5},{5,4},{6,7},{7,6},{8,9},{9,8},{10,11... | collective-permute-start | bytes 1179656 | tf_op jit(solution)/shard_map/ppermute | solution.py:175
  13.8 3.4 %collective-permute-start.7 = (f32[64,1024]{1,0:T(8,128)S(1)}, f32[64,1024]{1,0:T(8,128)S(1)}, u32[]{:S(2)}, u32[]{:S(2)}) collective-permute-start(f32[64,1024]{1,0:T(8,128)S(1)} %pad_maximum_fusion.2), channel_id=1, source_target_pairs={{0,4},{1,5},{2,6},{3,7},{4,0},{5,1},{6,2},{7,3},{8,12},{9,13},{10,... | collective-permute-start | bytes 786440 | tf_op jit(solution)/shard_map/ppermute | solution.py:175
  17.2 0.1 collective-permute-start.6
  17.3 0.0 collective-permute-done.9.s2_ref
  17.3 0.3 collective-permute-start.8
  17.6 0.0 collective-permute-done.4.near_ref.refs_1_
  17.6 0.0 copy-done.1
  17.6 3.8 %shard_map.56 = (bf16[2,512,512]{2,1,0:T(8,128)(2,1)S(1)}, f32[8,512]{1,0:T(8,128)S(1)}, f32[8,512]{1,0:T(8,128)S(1)}, f32[512,512]{1,0:T(8,128)S(1)}) custom-call(bf16[512,512]{1,0:T(8,128)(2,1)S(1)} %copy-done, bf16[512,512]{1,0:T(8,128)(2,1)S(1)} %copy-done.1, bf16[512,512]{1,0:T(8,128)(2,1)S(1)} %get-tuple-element.31.k_ref, ...), custom_call_target="tpu_custom_call" | custom-call | tf_op jit(solution)/shard_map/pallas_call | solution.py:24
  21.5 0.0 copy-start.2
  21.5 0.0 collective-permute-done.5.refs_7_
  21.5 4.6 %collective-permute-done.6.refs_2_ = f32[32,1024]{1,0:T(8,128)S(1)} collective-permute-done((f32[32,1024]{1,0:T(8,128)S(1)}, f32[32,1024]{1,0:T(8,128)S(1)}, u32[]{:S(2)}, u32[]{:S(2)}) %collective-permute-start.6) | collective-permute-done | bytes 131104 | tf_op jit(solution)/shard_map/ppermute | solution.py:175
  26.0 0.8 %collective-permute-done.8.refs_6_ = f32[32,1024]{1,0:T(8,128)S(1)} collective-permute-done((f32[32,1024]{1,0:T(8,128)S(1)}, f32[32,1024]{1,0:T(8,128)S(1)}, u32[]{:S(2)}, u32[]{:S(2)}) %collective-permute-start.8) | collective-permute-done | bytes 131104 | tf_op jit(solution)/shard_map/ppermute | solution.py:175
  26.8 0.0 collective-permute-done.7.refs_4_
  26.8 0.5 %collective-permute-start.10 = (f32[96,1024]{1,0:T(8,128)S(1)}, f32[96,1024]{1,0:T(8,128)S(1)}, u32[]{:S(2)}, u32[]{:S(2)}) collective-permute-start(f32[96,1024]{1,0:T(8,128)S(1)} %pad_maximum_fusion.1), channel_id=1, source_target_pairs={{0,1},{1,0},{2,3},{3,2},{4,5},{5,4},{6,7},{7,6},{8,9},{9,8},{10,11... | collective-permute-start | bytes 1179656 | tf_op jit(solution)/shard_map/ppermute | solution.py:175
  27.4 0.1 collective-permute-start.11
  27.5 1.6 %collective-permute-done.11.refs_5_ = f32[64,1024]{1,0:T(8,128)S(1)} collective-permute-done((f32[64,1024]{1,0:T(8,128)S(1)}, f32[64,1024]{1,0:T(8,128)S(1)}, u32[]{:S(2)}, u32[]{:S(2)}) %collective-permute-start.11) | collective-permute-done | bytes 262176 | tf_op jit(solution)/shard_map/ppermute | solution.py:175
  29.1 0.0 collective-permute-done.10.refs_3_
  29.1 0.0 copy-done.2
  29.1 3.2 %shard_map.57 = bf16[512,512]{1,0:T(8,128)(2,1)} custom-call(f32[32,1024]{1,0:T(8,128)S(1)} %constant_dynamic-update-slice_fusion.refs_0_, f32[96,1024]{1,0:T(8,128)S(1)} %collective-permute-done.4.near_ref.refs_1_, f32[32,1024]{1,0:T(8,128)S(1)} %collective-permute-done.6.refs_2_, f32[96,1024]{1,0:T(8,128)S(1)} %collective-permute-done.10.refs_3_, ...), custom_call_target="tpu_custom_call" | custom-call | tf_op jit(solution)/shard_map/pallas_call | solution.py:24
  (7 shorter events, 0.1 us)
Async XLA Ops:
  2.5 10.3 %collective-permute-start.3 = (f32[64,1024]{1,0:T(8,128)S(1)}, f32[64,1024]{1,0:T(8,128)S(1)}, u32[]{:S(2)}, u32[]{:S(2)}) collective-permute-start(f32[64,1024]{1,0:T(8,128)S(1)} %get-tuple-element.26), channel_id=1, source_target_pairs={{0,2},{1,3},{2,0},{3,1},{4,6},{5,7},{6,4},{7,5},{8,10},{9,11},{10,... | collective-permute-start | bytes 786440 | tf_op jit(solution)/shard_map/ppermute | solution.py:175
  5.1 2.3 %collective-permute-start.1 = (f32[8,1024]{1,0:T(8,128)S(1)}, f32[8,1024]{1,0:T(8,128)S(1)}, u32[]{:S(2)}, u32[]{:S(2)}) collective-permute-start(f32[8,1024]{1,0:T(8,128)S(1)} %get-tuple-element.25), channel_id=1, source_target_pairs={{0,1},{1,0},{2,3},{3,2},{4,5},{5,4},{6,7},{7,6},{8,9},{9,8},{10,11... | collective-permute-start | bytes 98312 | tf_op jit(solution)/shard_map/ppermute | solution.py:175
  6.0 6.8 %collective-permute-start = (f32[16,1024]{1,0:T(8,128)S(1)}, f32[16,1024]{1,0:T(8,128)S(1)}, u32[]{:S(2)}, u32[]{:S(2)}) collective-permute-start(f32[16,1024]{1,0:T(8,128)S(1)} %get-tuple-element.24), channel_id=1, source_target_pairs={{0,8},{1,9},{2,10},{3,11},{4,12},{5,13},{6,14},{7,15},{8,0},{9,1},... | collective-permute-start | bytes 196616 | tf_op jit(solution)/shard_map/ppermute | solution.py:175
  7.3 5.5 %collective-permute-start.2 = (f32[16,1024]{1,0:T(8,128)S(1)}, f32[16,1024]{1,0:T(8,128)S(1)}, u32[]{:S(2)}, u32[]{:S(2)}) collective-permute-start(f32[16,1024]{1,0:T(8,128)S(1)} %pad_maximum_fusion.3), channel_id=1, source_target_pairs={{0,16},{1,25},{2,18},{3,27},{4,20},{5,29},{6,22},{7,31},{8,24},{9,... | collective-permute-start | bytes 196616 | tf_op jit(solution)/shard_map/ppermute | solution.py:178
  9.6 7.7 %collective-permute-start.9 = (f32[128,1024]{1,0:T(8,128)S(1)}, f32[128,1024]{1,0:T(8,128)S(1)}, u32[]{:S(2)}, u32[]{:S(2)}) collective-permute-start(f32[128,1024]{1,0:T(8,128)S(1)} %get-tuple-element.33), channel_id=1, source_target_pairs={{0,1},{1,0},{2,3},{3,2},{4,5},{5,4},{6,7},{7,6},{8,9},{9,8},{10,11... | collective-permute-start | bytes 1572872 | tf_op jit(solution)/shard_map/ppermute | solution.py:175
  10.6 10.9 %collective-permute-start.5 = (f32[32,1024]{1,0:T(8,128)S(1)}, f32[32,1024]{1,0:T(8,128)S(1)}, u32[]{:S(2)}, u32[]{:S(2)}) collective-permute-start(f32[32,1024]{1,0:T(8,128)S(1)} %get-tuple-element.30), channel_id=1, source_target_pairs={{0,6},{1,7},{2,4},{3,5},{4,2},{5,3},{6,0},{7,1},{8,14},{9,15},{10,... | collective-permute-start | bytes 393224 | tf_op jit(solution)/shard_map/ppermute | solution.py:175
  12.9 4.8 %copy-start.1 = (bf16[512,512]{1,0:T(8,128)(2,1)S(1)}, bf16[512,512]{1,0:T(8,128)(2,1)}, u32[]{:S(2)}) copy-start(bf16[512,512]{1,0:T(8,128)(2,1)} %wq_ref.1) | copy-start | bytes 1572868
  12.9 4.7 %copy-start = (bf16[512,512]{1,0:T(8,128)(2,1)S(1)}, bf16[512,512]{1,0:T(8,128)(2,1)}, u32[]{:S(2)}) copy-start(bf16[512,512]{1,0:T(8,128)(2,1)} %x_ref.1) | copy-start | bytes 1572868
  12.9 4.7 %collective-permute-start.4 = (f32[96,1024]{1,0:T(8,128)S(1)}, f32[96,1024]{1,0:T(8,128)S(1)}, u32[]{:S(2)}, u32[]{:S(2)}) collective-permute-start(f32[96,1024]{1,0:T(8,128)S(1)} %pad_maximum_fusion), channel_id=1, source_target_pairs={{0,1},{1,0},{2,3},{3,2},{4,5},{5,4},{6,7},{7,6},{8,9},{9,8},{10,11... | collective-permute-start | bytes 1179656 | tf_op jit(solution)/shard_map/ppermute | solution.py:175
  13.8 13.0 %collective-permute-start.7 = (f32[64,1024]{1,0:T(8,128)S(1)}, f32[64,1024]{1,0:T(8,128)S(1)}, u32[]{:S(2)}, u32[]{:S(2)}) collective-permute-start(f32[64,1024]{1,0:T(8,128)S(1)} %pad_maximum_fusion.2), channel_id=1, source_target_pairs={{0,4},{1,5},{2,6},{3,7},{4,0},{5,1},{6,2},{7,3},{8,12},{9,13},{10,... | collective-permute-start | bytes 786440 | tf_op jit(solution)/shard_map/ppermute | solution.py:175
  17.2 8.8 %collective-permute-start.6 = (f32[32,1024]{1,0:T(8,128)S(1)}, f32[32,1024]{1,0:T(8,128)S(1)}, u32[]{:S(2)}, u32[]{:S(2)}) collective-permute-start(f32[32,1024]{1,0:T(8,128)S(1)} %constant_dynamic-update-slice_fusion.refs_0_), channel_id=1, source_target_pairs={{0,2},{1,3},{2,0},{3,1},{4,6},{5,7},{6,4},{7,5},{8,10},{9,11},{10,... | collective-permute-start | bytes 393224 | tf_op jit(solution)/shard_map/ppermute | solution.py:175
  17.3 9.5 %collective-permute-start.8 = (f32[32,1024]{1,0:T(8,128)S(1)}, f32[32,1024]{1,0:T(8,128)S(1)}, u32[]{:S(2)}, u32[]{:S(2)}) collective-permute-start(f32[32,1024]{1,0:T(8,128)S(1)} %constant_dynamic-update-slice_fusion.refs_0_), channel_id=1, source_target_pairs={{0,6},{1,7},{2,4},{3,5},{4,2},{5,3},{6,0},{7,1},{8,14},{9,15},{10,... | collective-permute-start | bytes 393224 | tf_op jit(solution)/shard_map/ppermute | solution.py:175
  21.5 7.7 %copy-start.2 = (bf16[512,512]{1,0:T(8,128)(2,1)S(1)}, bf16[512,512]{1,0:T(8,128)(2,1)}, u32[]{:S(2)}) copy-start(bf16[512,512]{1,0:T(8,128)(2,1)} %refs_12_.1) | copy-start | bytes 1572868
  26.8 2.3 %collective-permute-start.10 = (f32[96,1024]{1,0:T(8,128)S(1)}, f32[96,1024]{1,0:T(8,128)S(1)}, u32[]{:S(2)}, u32[]{:S(2)}) collective-permute-start(f32[96,1024]{1,0:T(8,128)S(1)} %pad_maximum_fusion.1), channel_id=1, source_target_pairs={{0,1},{1,0},{2,3},{3,2},{4,5},{5,4},{6,7},{7,6},{8,9},{9,8},{10,11... | collective-permute-start | bytes 1179656 | tf_op jit(solution)/shard_map/ppermute | solution.py:175
  27.4 1.7 %collective-permute-start.11 = (f32[64,1024]{1,0:T(8,128)S(1)}, f32[64,1024]{1,0:T(8,128)S(1)}, u32[]{:S(2)}, u32[]{:S(2)}) collective-permute-start(f32[64,1024]{1,0:T(8,128)S(1)} %collective-permute-done.7.refs_4_), channel_id=1, source_target_pairs={{0,1},{1,0},{2,3},{3,2},{4,5},{5,4},{6,7},{7,6},{8,9},{9,8},{10,11... | collective-permute-start | bytes 786440 | tf_op jit(solution)/shard_map/ppermute | solution.py:175

commit v6 on v4

--- a/solution.py
+++ b/solution.py
@@ -214,7 +214,7 @@
             pltpu.VMEM((2, D, BLK), BF16),
         ],
     )
-    z3, g1, g2, g3, top = lax.optimization_barrier((z3, g1, g2, g3, top))
+    g1, g2, g3, top = lax.optimization_barrier((g1, g2, g3, top))
     zf = swap(z3, 1)
     def staged(slots):
         return [pltpu.VMEM((slots, BLK, D), BF16), pltpu.VMEM((slots, D, BLK), BF16)]

time: 32.4 us -> 34.9 us (1.077)
  starting transfers between devices: 16 us -> 17.8 us
  waiting for transfers between devices: 6.66 us -> 7.35 us
    ppermute x13, starting transfers between devices: 13.7 us -> 15.5 us  [swap(): return lax.ppermute(block, 'seq', [(i, i ^ apart) for i in range(count)])]
    ppermute x1, waiting for transfers between devices: 0.01 us -> 1.15 us  [beyond(): lax.ppermute(block, 'seq', [(i, i ^ (24 if i & 1 else 16)) for i in range...]
    ppermute x13, waiting for transfers between devices: 6.66 us -> 6.2 us  [swap(): return lax.ppermute(block, 'seq', [(i, i ^ apart) for i in range(count)])]
  transfers between devices with their start and end apart: 14 -> 14, of which waited for: 5 -> 7; matrix products, arithmetic and copies ran while one was open for 0% -> 0% of each run, Pallas kernels for 12% -> 11%
where the time goes in v6:
time: 34.9 us; the launch traced here: 34.8 us
  starting transfers between devices  17.8 us (51%)
  Pallas kernels  9.5 us (27%)
  waiting for transfers between devices  7.35 us (21%)
    ppermute x13, starting transfers between devices, swap(): return lax.ppermute(block, 'seq', [(i, i ^ apart) for i in range(count)])  15.5 us
    pallas_call x3, Pallas kernels, call(): pl.pallas_call(body, out_shape=outs, in_specs=[place] * len(args), out_sp...  9.5 us
    ppermute x13, waiting for transfers between devices, swap(): return lax.ppermute(block, 'seq', [(i, i ^ apart) for i in range(count)])  6.2 us
    ppermute x1, starting transfers between devices, beyond(): lax.ppermute(block, 'seq', [(i, i ^ (24 if i & 1 else 16)) for i in range...  2.28 us
    ppermute x1, waiting for transfers between devices, beyond(): lax.ppermute(block, 'seq', [(i, i ^ (24 if i & 1 else 16)) for i in range...  1.15 us
  transfers between devices with their start and end apart: 14, of which 7 were waited for; matrix products, arithmetic and copies ran while one was open for 0% of the time, Pallas kernels for 11%

profile of v6, /device:TPU:1, one launch (start us, length us, event | category | flops | bytes accessed | tf_op | source)
XLA Modules:
  0.0 34.8 jit_solution(10066444115468859890)
XLA Ops:
  0.0 2.5 %shard_map.55 = (bf16[512,512]{1,0:T(8,128)(2,1)S(1)}, bf16[512,512]{1,0:T(8,128)(2,1)S(1)}, f32[128,1024]{1,0:T(8,128)S(1)}, f32[64,1024]{1,0:T(8,128)S(1)}, f3...) custom-call(bf16[512,512]{1,0:T(8,128)(2,1)} %x_ref.1, bf16[512,512]{1,0:T(8,128)(2,1)} %wk_hbm.1, ...), custom_call_target="tpu_custom_call" | custom-call | tf_op jit(solution)/shard_map/pallas_call | solution.py:24
  2.5 2.5 %collective-permute-start.3 = (f32[64,1024]{1,0:T(8,128)S(1)}, f32[64,1024]{1,0:T(8,128)S(1)}, u32[]{:S(2)}, u32[]{:S(2)}) collective-permute-start(f32[64,1024]{1,0:T(8,128)S(1)} %get-tuple-element.25), channel_id=1, source_target_pairs={{0,2},{1,3},{2,0},{3,1},{4,6},{5,7},{6,4},{7,5},{8,10},{9,11},{10,... | collective-permute-start | bytes 786440 | tf_op jit(solution)/shard_map/ppermute | solution.py:175
  5.1 1.0 %collective-permute-start.1 = (f32[8,1024]{1,0:T(8,128)S(1)}, f32[8,1024]{1,0:T(8,128)S(1)}, u32[]{:S(2)}, u32[]{:S(2)}) collective-permute-start(f32[8,1024]{1,0:T(8,128)S(1)} %get-tuple-element.24), channel_id=1, source_target_pairs={{0,1},{1,0},{2,3},{3,2},{4,5},{5,4},{6,7},{7,6},{8,9},{9,8},{10,11... | collective-permute-start | bytes 98312 | tf_op jit(solution)/shard_map/ppermute | solution.py:175
  6.0 1.3 %collective-permute-start = (f32[16,1024]{1,0:T(8,128)S(1)}, f32[16,1024]{1,0:T(8,128)S(1)}, u32[]{:S(2)}, u32[]{:S(2)}) collective-permute-start(f32[16,1024]{1,0:T(8,128)S(1)} %get-tuple-element.23), channel_id=1, source_target_pairs={{0,8},{1,9},{2,10},{3,11},{4,12},{5,13},{6,14},{7,15},{8,0},{9,1},... | collective-permute-start | bytes 196616 | tf_op jit(solution)/shard_map/ppermute | solution.py:175
  7.3 0.0 collective-permute-done.1
  7.3 2.3 %collective-permute-start.2 = (f32[16,1024]{1,0:T(8,128)S(1)}, f32[16,1024]{1,0:T(8,128)S(1)}, u32[]{:S(2)}, u32[]{:S(2)}) collective-permute-start(f32[16,1024]{1,0:T(8,128)S(1)} %pad_maximum_fusion.2), channel_id=1, source_target_pairs={{0,16},{1,25},{2,18},{3,27},{4,20},{5,29},{6,22},{7,31},{8,24},{9,... | collective-permute-start | bytes 196616 | tf_op jit(solution)/shard_map/ppermute | solution.py:178
  9.6 1.0 %collective-permute-start.8 = (f32[128,1024]{1,0:T(8,128)S(1)}, f32[128,1024]{1,0:T(8,128)S(1)}, u32[]{:S(2)}, u32[]{:S(2)}) collective-permute-start(f32[128,1024]{1,0:T(8,128)S(1)} %get-tuple-element.32), channel_id=1, source_target_pairs={{0,1},{1,0},{2,3},{3,2},{4,5},{5,4},{6,7},{7,6},{8,9},{9,8},{10,11... | collective-permute-start | bytes 1572872 | tf_op jit(solution)/shard_map/ppermute | solution.py:175
  10.6 0.0 collective-permute-done
  10.6 1.1 %collective-permute-done.2 = f32[16,1024]{1,0:T(8,128)S(1)} collective-permute-done((f32[16,1024]{1,0:T(8,128)S(1)}, f32[16,1024]{1,0:T(8,128)S(1)}, u32[]{:S(2)}, u32[]{:S(2)}) %collective-permute-start.2) | collective-permute-done | bytes 65568 | tf_op jit(solution)/shard_map/ppermute | solution.py:178
  11.7 0.0 collective-permute-done.3.z1_ref
  11.8 0.0 copy-start
  11.8 2.0 %collective-permute-start.4 = (f32[96,1024]{1,0:T(8,128)S(1)}, f32[96,1024]{1,0:T(8,128)S(1)}, u32[]{:S(2)}, u32[]{:S(2)}) collective-permute-start(f32[96,1024]{1,0:T(8,128)S(1)} %pad_maximum_fusion), channel_id=1, source_target_pairs={{0,1},{1,0},{2,3},{3,2},{4,5},{5,4},{6,7},{7,6},{8,9},{9,8},{10,11... | collective-permute-start | bytes 1179656 | tf_op jit(solution)/shard_map/ppermute | solution.py:175
  13.8 3.4 %collective-permute-start.6 = (f32[64,1024]{1,0:T(8,128)S(1)}, f32[64,1024]{1,0:T(8,128)S(1)}, u32[]{:S(2)}, u32[]{:S(2)}) collective-permute-start(f32[64,1024]{1,0:T(8,128)S(1)} %pad_maximum_fusion.1), channel_id=1, source_target_pairs={{0,4},{1,5},{2,6},{3,7},{4,0},{5,1},{6,2},{7,3},{8,12},{9,13},{10,... | collective-permute-start | bytes 786440 | tf_op jit(solution)/shard_map/ppermute | solution.py:175
  17.2 0.1 collective-permute-start.5
  17.3 0.3 collective-permute-start.7
  17.6 0.0 collective-permute-done.8.s2_ref
  17.6 2.5 %collective-permute-start.12 = (f32[32,1024]{1,0:T(8,128)S(1)}, f32[32,1024]{1,0:T(8,128)S(1)}, u32[]{:S(2)}, u32[]{:S(2)}) collective-permute-start(f32[32,1024]{1,0:T(8,128)S(1)} %get-tuple-element.29), channel_id=1, source_target_pairs={{0,6},{1,7},{2,4},{3,5},{4,2},{5,3},{6,0},{7,1},{8,14},{9,15},{10,... | collective-permute-start | bytes 393224 | tf_op jit(solution)/shard_map/ppermute | solution.py:175
  20.1 0.0 collective-permute-done.4.near_ref.refs_1_
  20.1 0.0 copy-start.2
  20.1 3.8 %shard_map.56 = (bf16[2,512,512]{2,1,0:T(8,128)(2,1)S(1)}, f32[8,512]{1,0:T(8,128)S(1)}, f32[8,512]{1,0:T(8,128)S(1)}, f32[512,512]{1,0:T(8,128)S(1)}) custom-call(bf16[512,512]{1,0:T(8,128)(2,1)S(1)} %copy-done, bf16[512,512]{1,0:T(8,128)(2,1)S(1)} %copy-done.1, bf16[512,512]{1,0:T(8,128)(2,1)S(1)} %get-tuple-element.30.k_ref, ...), custom_call_target="tpu_custom_call" | custom-call | tf_op jit(solution)/shard_map/pallas_call | solution.py:24
  23.9 2.1 %collective-permute-done.5.refs_2_ = f32[32,1024]{1,0:T(8,128)S(1)} collective-permute-done((f32[32,1024]{1,0:T(8,128)S(1)}, f32[32,1024]{1,0:T(8,128)S(1)}, u32[]{:S(2)}, u32[]{:S(2)}) %collective-permute-start.5) | collective-permute-done | bytes 131104 | tf_op jit(solution)/shard_map/ppermute | solution.py:175
  26.0 0.8 %collective-permute-done.7.refs_6_ = f32[32,1024]{1,0:T(8,128)S(1)} collective-permute-done((f32[32,1024]{1,0:T(8,128)S(1)}, f32[32,1024]{1,0:T(8,128)S(1)}, u32[]{:S(2)}, u32[]{:S(2)}) %collective-permute-start.7) | collective-permute-done | bytes 131104 | tf_op jit(solution)/shard_map/ppermute | solution.py:175
  26.8 0.5 %collective-permute-start.10 = (f32[64,1024]{1,0:T(8,128)S(1)}, f32[64,1024]{1,0:T(8,128)S(1)}, u32[]{:S(2)}, u32[]{:S(2)}) collective-permute-start(f32[64,1024]{1,0:T(8,128)S(1)} %collective-permute-done.6.refs_4_), channel_id=1, source_target_pairs={{0,1},{1,0},{2,3},{3,2},{4,5},{5,4},{6,7},{7,6},{8,9},{9,8},{10,11... | collective-permute-start | bytes 786440 | tf_op jit(solution)/shard_map/ppermute | solution.py:175
  27.4 2.3 %collective-permute-done.12.refs_8_ = f32[32,1024]{1,0:T(8,128)S(1)} collective-permute-done((f32[32,1024]{1,0:T(8,128)S(1)}, f32[32,1024]{1,0:T(8,128)S(1)}, u32[]{:S(2)}, u32[]{:S(2)}) %collective-permute-start.12) | collective-permute-done | bytes 131104 | tf_op jit(solution)/shard_map/ppermute | solution.py:175
  29.6 0.5 %collective-permute-start.13 = (f32[32,1024]{1,0:T(8,128)S(1)}, f32[32,1024]{1,0:T(8,128)S(1)}, u32[]{:S(2)}, u32[]{:S(2)}) collective-permute-start(f32[32,1024]{1,0:T(8,128)S(1)} %collective-permute-done.12.refs_8_), channel_id=1, source_target_pairs={{0,1},{1,0},{2,3},{3,2},{4,5},{5,4},{6,7},{7,6},{8,9},{9,8},{10,11... | collective-permute-start | bytes 393224 | tf_op jit(solution)/shard_map/ppermute | solution.py:175
  30.1 0.0 collective-permute-start.11
  30.1 0.5 %collective-permute-start.9 = (f32[32,1024]{1,0:T(8,128)S(1)}, f32[32,1024]{1,0:T(8,128)S(1)}, u32[]{:S(2)}, u32[]{:S(2)}) collective-permute-start(f32[32,1024]{1,0:T(8,128)S(1)} %collective-permute-done.5.refs_2_), channel_id=1, source_target_pairs={{0,1},{1,0},{2,3},{3,2},{4,5},{5,4},{6,7},{7,6},{8,9},{9,8},{10,11... | collective-permute-start | bytes 393224 | tf_op jit(solution)/shard_map/ppermute | solution.py:175
  30.6 0.5 %collective-permute-done.13.refs_9_ = f32[32,1024]{1,0:T(8,128)S(1)} collective-permute-done((f32[32,1024]{1,0:T(8,128)S(1)}, f32[32,1024]{1,0:T(8,128)S(1)}, u32[]{:S(2)}, u32[]{:S(2)}) %collective-permute-start.13) | collective-permute-done | bytes 131104 | tf_op jit(solution)/shard_map/ppermute | solution.py:175
  31.1 0.4 %collective-permute-done.11.refs_7_ = f32[32,1024]{1,0:T(8,128)S(1)} collective-permute-done((f32[32,1024]{1,0:T(8,128)S(1)}, f32[32,1024]{1,0:T(8,128)S(1)}, u32[]{:S(2)}, u32[]{:S(2)}) %collective-permute-start.11) | collective-permute-done | bytes 131104 | tf_op jit(solution)/shard_map/ppermute | solution.py:175
  31.4 0.2 collective-permute-done.9.refs_3_
  31.6 0.0 collective-permute-done.10.refs_5_
  31.6 3.2 %shard_map.57 = bf16[512,512]{1,0:T(8,128)(2,1)} custom-call(f32[32,1024]{1,0:T(8,128)S(1)} %constant_dynamic-update-slice_fusion.refs_0_, f32[96,1024]{1,0:T(8,128)S(1)} %collective-permute-done.4.near_ref.refs_1_, f32[32,1024]{1,0:T(8,128)S(1)} %collective-permute-done.5.refs_2_, f32[32,1024]{1,0:T(8,128)S(1)} %collective-permute-done.9.refs_3_, ...), custom_call_target="tpu_custom_call" | custom-call | tf_op jit(solution)/shard_map/pallas_call | solution.py:24
  (10 shorter events, 0.1 us)
Async XLA Ops:
  2.5 9.2 %collective-permute-start.3 = (f32[64,1024]{1,0:T(8,128)S(1)}, f32[64,1024]{1,0:T(8,128)S(1)}, u32[]{:S(2)}, u32[]{:S(2)}) collective-permute-start(f32[64,1024]{1,0:T(8,128)S(1)} %get-tuple-element.25), channel_id=1, source_target_pairs={{0,2},{1,3},{2,0},{3,1},{4,6},{5,7},{6,4},{7,5},{8,10},{9,11},{10,... | collective-permute-start | bytes 786440 | tf_op jit(solution)/shard_map/ppermute | solution.py:175
  5.1 2.3 %collective-permute-start.1 = (f32[8,1024]{1,0:T(8,128)S(1)}, f32[8,1024]{1,0:T(8,128)S(1)}, u32[]{:S(2)}, u32[]{:S(2)}) collective-permute-start(f32[8,1024]{1,0:T(8,128)S(1)} %get-tuple-element.24), channel_id=1, source_target_pairs={{0,1},{1,0},{2,3},{3,2},{4,5},{5,4},{6,7},{7,6},{8,9},{9,8},{10,11... | collective-permute-start | bytes 98312 | tf_op jit(solution)/shard_map/ppermute | solution.py:175
  6.0 4.6 %collective-permute-start = (f32[16,1024]{1,0:T(8,128)S(1)}, f32[16,1024]{1,0:T(8,128)S(1)}, u32[]{:S(2)}, u32[]{:S(2)}) collective-permute-start(f32[16,1024]{1,0:T(8,128)S(1)} %get-tuple-element.23), channel_id=1, source_target_pairs={{0,8},{1,9},{2,10},{3,11},{4,12},{5,13},{6,14},{7,15},{8,0},{9,1},... | collective-permute-start | bytes 196616 | tf_op jit(solution)/shard_map/ppermute | solution.py:175
  7.3 4.4 %collective-permute-start.2 = (f32[16,1024]{1,0:T(8,128)S(1)}, f32[16,1024]{1,0:T(8,128)S(1)}, u32[]{:S(2)}, u32[]{:S(2)}) collective-permute-start(f32[16,1024]{1,0:T(8,128)S(1)} %pad_maximum_fusion.2), channel_id=1, source_target_pairs={{0,16},{1,25},{2,18},{3,27},{4,20},{5,29},{6,22},{7,31},{8,24},{9,... | collective-permute-start | bytes 196616 | tf_op jit(solution)/shard_map/ppermute | solution.py:178
  9.6 8.0 %collective-permute-start.8 = (f32[128,1024]{1,0:T(8,128)S(1)}, f32[128,1024]{1,0:T(8,128)S(1)}, u32[]{:S(2)}, u32[]{:S(2)}) collective-permute-start(f32[128,1024]{1,0:T(8,128)S(1)} %get-tuple-element.32), channel_id=1, source_target_pairs={{0,1},{1,0},{2,3},{3,2},{4,5},{5,4},{6,7},{7,6},{8,9},{9,8},{10,11... | collective-permute-start | bytes 1572872 | tf_op jit(solution)/shard_map/ppermute | solution.py:175
  11.8 8.3 %copy-start.1 = (bf16[512,512]{1,0:T(8,128)(2,1)S(1)}, bf16[512,512]{1,0:T(8,128)(2,1)}, u32[]{:S(2)}) copy-start(bf16[512,512]{1,0:T(8,128)(2,1)} %wq_ref.1) | copy-start | bytes 1572868
  11.8 8.3 %copy-start = (bf16[512,512]{1,0:T(8,128)(2,1)S(1)}, bf16[512,512]{1,0:T(8,128)(2,1)}, u32[]{:S(2)}) copy-start(bf16[512,512]{1,0:T(8,128)(2,1)} %x_ref.1) | copy-start | bytes 1572868
  11.8 8.3 %collective-permute-start.4 = (f32[96,1024]{1,0:T(8,128)S(1)}, f32[96,1024]{1,0:T(8,128)S(1)}, u32[]{:S(2)}, u32[]{:S(2)}) collective-permute-start(f32[96,1024]{1,0:T(8,128)S(1)} %pad_maximum_fusion), channel_id=1, source_target_pairs={{0,1},{1,0},{2,3},{3,2},{4,5},{5,4},{6,7},{7,6},{8,9},{9,8},{10,11... | collective-permute-start | bytes 1179656 | tf_op jit(solution)/shard_map/ppermute | solution.py:175
  13.8 13.0 %collective-permute-start.6 = (f32[64,1024]{1,0:T(8,128)S(1)}, f32[64,1024]{1,0:T(8,128)S(1)}, u32[]{:S(2)}, u32[]{:S(2)}) collective-permute-start(f32[64,1024]{1,0:T(8,128)S(1)} %pad_maximum_fusion.1), channel_id=1, source_target_pairs={{0,4},{1,5},{2,6},{3,7},{4,0},{5,1},{6,2},{7,3},{8,12},{9,13},{10,... | collective-permute-start | bytes 786440 | tf_op jit(solution)/shard_map/ppermute | solution.py:175
  17.2 8.8 %collective-permute-start.5 = (f32[32,1024]{1,0:T(8,128)S(1)}, f32[32,1024]{1,0:T(8,128)S(1)}, u32[]{:S(2)}, u32[]{:S(2)}) collective-permute-start(f32[32,1024]{1,0:T(8,128)S(1)} %constant_dynamic-update-slice_fusion.refs_0_), channel_id=1, source_target_pairs={{0,2},{1,3},{2,0},{3,1},{4,6},{5,7},{6,4},{7,5},{8,10},{9,11},{10,... | collective-permute-start | bytes 393224 | tf_op jit(solution)/shard_map/ppermute | solution.py:175
  17.3 9.5 %collective-permute-start.7 = (f32[32,1024]{1,0:T(8,128)S(1)}, f32[32,1024]{1,0:T(8,128)S(1)}, u32[]{:S(2)}, u32[]{:S(2)}) collective-permute-start(f32[32,1024]{1,0:T(8,128)S(1)} %constant_dynamic-update-slice_fusion.refs_0_), channel_id=1, source_target_pairs={{0,6},{1,7},{2,4},{3,5},{4,2},{5,3},{6,0},{7,1},{8,14},{9,15},{10,... | collective-permute-start | bytes 393224 | tf_op jit(solution)/shard_map/ppermute | solution.py:175
  17.6 12.0 %collective-permute-start.12 = (f32[32,1024]{1,0:T(8,128)S(1)}, f32[32,1024]{1,0:T(8,128)S(1)}, u32[]{:S(2)}, u32[]{:S(2)}) collective-permute-start(f32[32,1024]{1,0:T(8,128)S(1)} %get-tuple-element.29), channel_id=1, source_target_pairs={{0,6},{1,7},{2,4},{3,5},{4,2},{5,3},{6,0},{7,1},{8,14},{9,15},{10,... | collective-permute-start | bytes 393224 | tf_op jit(solution)/shard_map/ppermute | solution.py:175
  20.1 11.5 %copy-start.2 = (bf16[512,512]{1,0:T(8,128)(2,1)S(1)}, bf16[512,512]{1,0:T(8,128)(2,1)}, u32[]{:S(2)}) copy-start(bf16[512,512]{1,0:T(8,128)(2,1)} %refs_14_.1) | copy-start | bytes 1572868
  26.8 4.8 %collective-permute-start.10 = (f32[64,1024]{1,0:T(8,128)S(1)}, f32[64,1024]{1,0:T(8,128)S(1)}, u32[]{:S(2)}, u32[]{:S(2)}) collective-permute-start(f32[64,1024]{1,0:T(8,128)S(1)} %collective-permute-done.6.refs_4_), channel_id=1, source_target_pairs={{0,1},{1,0},{2,3},{3,2},{4,5},{5,4},{6,7},{7,6},{8,9},{9,8},{10,11... | collective-permute-start | bytes 786440 | tf_op jit(solution)/shard_map/ppermute | solution.py:175
  29.6 1.5 %collective-permute-start.13 = (f32[32,1024]{1,0:T(8,128)S(1)}, f32[32,1024]{1,0:T(8,128)S(1)}, u32[]{:S(2)}, u32[]{:S(2)}) collective-permute-start(f32[32,1024]{1,0:T(8,128)S(1)} %collective-permute-done.12.refs_8_), channel_id=1, source_target_pairs={{0,1},{1,0},{2,3},{3,2},{4,5},{5,4},{6,7},{7,6},{8,9},{9,8},{10,11... | collective-permute-start | bytes 393224 | tf_op jit(solution)/shard_map/ppermute | solution.py:175
  30.1 1.3 %collective-permute-start.11 = (f32[32,1024]{1,0:T(8,128)S(1)}, f32[32,1024]{1,0:T(8,128)S(1)}, u32[]{:S(2)}, u32[]{:S(2)}) collective-permute-start(f32[32,1024]{1,0:T(8,128)S(1)} %collective-permute-done.7.refs_6_), channel_id=1, source_target_pairs={{0,1},{1,0},{2,3},{3,2},{4,5},{5,4},{6,7},{7,6},{8,9},{9,8},{10,11... | collective-permute-start | bytes 393224 | tf_op jit(solution)/shard_map/ppermute | solution.py:175
  30.1 1.5 %collective-permute-start.9 = (f32[32,1024]{1,0:T(8,128)S(1)}, f32[32,1024]{1,0:T(8,128)S(1)}, u32[]{:S(2)}, u32[]{:S(2)}) collective-permute-start(f32[32,1024]{1,0:T(8,128)S(1)} %collective-permute-done.5.refs_2_), channel_id=1, source_target_pairs={{0,1},{1,0},{2,3},{3,2},{4,5},{5,4},{6,7},{7,6},{8,9},{9,8},{10,11... | collective-permute-start | bytes 393224 | tf_op jit(solution)/shard_map/ppermute | solution.py:175
